TPU v7x, 32 devices: a whole 2x2x4 slice. The times are simulated.
32 devices in a mesh: section: 2 (over core), shard: 4 (over z), rep: 4 (over y, x).
Axes of the slice: x: 2, y: 2, z: 4, core: 2. Of those that a mesh axis runs over, the one named last changes fastest.
Arguments:
- images: bfloat16 [4, 32, 196, 512], P(None, ('shard', 'rep')), may hold values from -6 to 6
- cotangent: bfloat16 [4, 32, 196, 512], P(None, ('shard', 'rep')), may hold values from -6 to 6
- region: int32 [196], replicated, may hold values from 0 to 3
- rel_index: int32 [49, 49], replicated, may hold values from 0 to 168
- norm1_gain: float32 [2, 512], P('section'), may hold values from 0.5 to 1.5
- norm1_bias: float32 [2, 512], P('section'), may hold values from -1.25 to 1.25
- w_qkv: bfloat16 [2, 512, 1536], P('section', 'shard'), may hold values from -0.25 to 0.25
- qv_bias: float32 [2, 1024], P('section'), may hold values from -1.25 to 1.25
- rel_table: float32 [2, 169, 16], P('section'), may hold values from -6 to 6
- w_proj: bfloat16 [2, 512, 512], P('section', 'shard'), may hold values from -0.75 to 0.75
- proj_bias: float32 [2, 512], P('section'), may hold values from -1.25 to 1.25
- norm2_gain: float32 [2, 512], P('section'), may hold values from 0.5 to 1.5
- norm2_bias: float32 [2, 512], P('section'), may hold values from -1.25 to 1.25
- w_fc1: bfloat16 [2, 512, 2048], P('section', 'shard'), may hold values from -0.25 to 0.25
- fc1_bias: float32 [2, 2048], P('section'), may hold values from -1.25 to 1.25
- w_fc2: bfloat16 [2, 2048, 512], P('section', 'shard'), may hold values from -0.125 to 0.125
- fc2_bias: float32 [2, 512], P('section'), may hold values from -1.25 to 1.25
Outputs:
- section_out: bfloat16 [2, 4, 32, 196, 512], P('section', None, ('shard', 'rep'))
- input_grad: float32 [2, 4, 32, 196, 512], P('section', None, ('shard', 'rep'))
- grad_norm1_gain: float32 [2, 512], P('section')
- grad_norm1_bias: float32 [2, 512], P('section')
- grad_qkv: float32 [2, 512, 1536], P('section', 'shard')
- grad_qv_bias: float32 [2, 1024], P('section')
- grad_table: float32 [2, 169, 16], P('section')
- grad_proj: float32 [2, 512, 512], P('section', 'shard')
- grad_proj_bias: float32 [2, 512], P('section')
- grad_norm2_gain: float32 [2, 512], P('section')
- grad_norm2_bias: float32 [2, 512], P('section')
- grad_fc1: float32 [2, 512, 2048], P('section', 'shard')
- grad_fc1_bias: float32 [2, 2048], P('section')
- grad_fc2: float32 [2, 2048, 512], P('section', 'shard')
- grad_fc2_bias: float32 [2, 512], P('section')
All inputs are finite; a program needn't handle non-finite values.
Results may differ from a plain program's by a relative error of at most 0.023.
Values may be sent and summed in bfloat16 or wider, within the bound.
A program may use at most 256 MiB of HBM per device.

v0:
```python
import math

import jax
import jax.numpy as jnp
from jax import lax
from jax.sharding import PartitionSpec as P

HEAD = 32
WIN = 7
GRID = 14
SHIFT = 3


def shifted(block, axis, distance):
    devices = range(lax.axis_size(axis))
    route = [(i - distance, i) for i in devices if i - distance in devices]
    return lax.ppermute(block, axis, route)


def shortened(value):

    def short(part):
        return part.astype(jnp.bfloat16) if part.dtype == jnp.float32 else part

    return jax.tree.map(short, value)


def flat_rows(tensor):
    return tensor.reshape(-1, tensor.shape[-1])


def times_plain(left, matrix):
    result = jnp.dot(flat_rows(left), matrix, preferred_element_type=jnp.float32)
    return result.reshape(left.shape[:-1] + (matrix.shape[1],))


def times_trans(left, matrix):
    result = lax.dot_general(
        flat_rows(left), matrix, (((1,), (1,)), ((), ())), preferred_element_type=jnp.float32
    )
    return result.reshape(left.shape[:-1] + (matrix.shape[0],))


def outer_sum(left, right):
    return lax.dot_general(
        flat_rows(left),
        flat_rows(right),
        (((0,), (0,)), ((), ())),
        preferred_element_type=jnp.float32,
    )


def norm_forward(values, gain, beta_term):
    average = jnp.mean(values, -1, keepdims=True)
    centred = values - average
    inverse = lax.rsqrt(jnp.mean(centred * centred, -1, keepdims=True) + 1e-05)
    unit_rows = centred * inverse
    return (unit_rows * gain + beta_term, unit_rows, inverse)


def norm_backward(grad_in, unit_rows, inverse, gain):
    scaled = grad_in * gain
    grad_values = inverse * (
        scaled
        - jnp.mean(scaled, -1, keepdims=True)
        - unit_rows * jnp.mean(scaled * unit_rows, -1, keepdims=True)
    )
    return (grad_values, jnp.sum(grad_in * unit_rows, axis=(0, 1)), jnp.sum(grad_in, axis=(0, 1)))


def gelu_slope(values):
    cumulative = 0.5 * (1.0 + lax.erf(values * (1.0 / math.sqrt(2.0))))
    density = jnp.exp(-0.5 * values * values) * (1.0 / math.sqrt(2.0 * math.pi))
    return cumulative + values * density


def to_windows(tensor, offset):
    images_here, tokens_here, channels = tensor.shape
    per_side = GRID // WIN
    lattice = tensor.reshape(images_here, GRID, GRID, channels)
    lattice = jnp.roll(lattice, (-offset, -offset), (1, 2))
    lattice = lattice.reshape(images_here, per_side, WIN, per_side, WIN, channels).transpose(
        0, 1, 3, 2, 4, 5
    )
    return lattice.reshape(images_here * per_side * per_side, WIN * WIN, channels)


def from_windows(tensor, offset, images_here):
    channels = tensor.shape[-1]
    per_side = GRID // WIN
    lattice = tensor.reshape(images_here, per_side, per_side, WIN, WIN, channels).transpose(
        0, 1, 3, 2, 4, 5
    )
    lattice = lattice.reshape(images_here, GRID, GRID, channels)
    lattice = jnp.roll(lattice, (offset, offset), (1, 2))
    return lattice.reshape(images_here, GRID * GRID, channels)


def layer_forward(inputs, small, mats, offset, mask_add, rel_bias):
    norm1_gain, norm1_bias, qv_bias, proj_bias, norm2_gain, norm2_bias, fc1_bias, fc2_bias = small
    w_qkv, w_proj, w_fc1, w_fc2 = mats
    images_here = inputs.shape[0]
    channels = inputs.shape[-1]
    heads_all = channels // HEAD
    scale_qk = 1.0 / math.sqrt(HEAD)
    normed, unit_one, inverse_one = norm_forward(inputs, norm1_gain, norm1_bias)
    normed_low = normed.astype(jnp.bfloat16)
    full_bias = jnp.concatenate(
        [qv_bias[:channels], jnp.zeros((channels,), jnp.float32), qv_bias[channels:]]
    )
    projected = (times_plain(normed_low, w_qkv) + full_bias).astype(jnp.bfloat16)
    windowed = to_windows(projected, offset)
    win_count = windowed.shape[0]
    split_up = windowed.reshape(win_count, WIN * WIN, 3, heads_all, HEAD)
    win_q = split_up[:, :, 0]
    win_k = split_up[:, :, 1]
    win_v = split_up[:, :, 2]
    scores = (
        jnp.einsum("wihd,wjhd->whij", win_q, win_k, preferred_element_type=jnp.float32) * scale_qk
    )
    scores = scores + rel_bias[None]
    scores = (
        scores.reshape(images_here, -1, heads_all, WIN * WIN, WIN * WIN) + mask_add[None, :, None]
    ).reshape(scores.shape)
    highest = jnp.max(scores, -1, keepdims=True)
    expo_s = jnp.exp(scores - highest)
    probs = expo_s / jnp.sum(expo_s, -1, keepdims=True)
    probs_low = probs.astype(jnp.bfloat16)
    attended = jnp.einsum("whij,wjhd->wihd", probs_low, win_v, preferred_element_type=jnp.float32)
    attended = attended.astype(jnp.bfloat16)
    merged = from_windows(attended.reshape(win_count, WIN * WIN, channels), offset, images_here)
    middle = inputs + (times_plain(merged, w_proj) + proj_bias)
    normed_two, unit_two, inverse_two = norm_forward(middle, norm2_gain, norm2_bias)
    normed_two_low = normed_two.astype(jnp.bfloat16)
    hidden = times_plain(normed_two_low, w_fc1) + fc1_bias
    activated = jax.nn.gelu(hidden, approximate=False).astype(jnp.bfloat16)
    output = middle + (times_plain(activated, w_fc2) + fc2_bias)
    saved = (
        unit_one,
        inverse_one,
        normed_low,
        win_q,
        win_k,
        win_v,
        probs,
        probs_low,
        merged,
        unit_two,
        inverse_two,
        normed_two_low,
        hidden,
        activated,
    )
    return (output, saved)


def layer_backward(inputs, grad_out, small, mats, offset, mask_add, rel_bias, onehot):
    norm1_gain, norm1_bias, qv_bias, proj_bias, norm2_gain, norm2_bias, fc1_bias, fc2_bias = small
    w_qkv, w_proj, w_fc1, w_fc2 = mats
    output, saved = layer_forward(inputs, small, mats, offset, mask_add, rel_bias)
    (
        unit_one,
        inverse_one,
        normed_low,
        win_q,
        win_k,
        win_v,
        probs,
        probs_low,
        merged,
        unit_two,
        inverse_two,
        normed_two_low,
        hidden,
        activated,
    ) = saved
    images_here = inputs.shape[0]
    channels = inputs.shape[-1]
    heads_all = channels // HEAD
    scale_qk = 1.0 / math.sqrt(HEAD)
    win_count = win_q.shape[0]
    grad_two_low = grad_out.astype(jnp.bfloat16)
    grad_fc2 = outer_sum(activated, grad_two_low)
    grad_fc2_bias = jnp.sum(grad_two_low, axis=(0, 1), dtype=jnp.float32)
    grad_act = times_trans(grad_two_low, w_fc2)
    grad_hidden = (grad_act * gelu_slope(hidden)).astype(jnp.bfloat16)
    grad_fc1 = outer_sum(normed_two_low, grad_hidden)
    grad_fc1_bias = jnp.sum(grad_hidden, axis=(0, 1), dtype=jnp.float32)
    grad_normed_two = times_trans(grad_hidden, w_fc1)
    grad_mid_norm, grad_gain_two, grad_beta_two = norm_backward(
        grad_normed_two, unit_two, inverse_two, norm2_gain
    )
    grad_middle = grad_out + grad_mid_norm
    grad_branch_low = grad_middle.astype(jnp.bfloat16)
    grad_proj = outer_sum(merged, grad_branch_low)
    grad_proj_bias = jnp.sum(grad_branch_low, axis=(0, 1), dtype=jnp.float32)
    grad_merged = times_trans(grad_branch_low, w_proj).astype(jnp.bfloat16)
    grad_att = to_windows(grad_merged, offset).reshape(win_count, WIN * WIN, heads_all, HEAD)
    grad_probs = jnp.einsum("wihd,wjhd->whij", grad_att, win_v, preferred_element_type=jnp.float32)
    grad_vals = jnp.einsum(
        "whij,wihd->wjhd", probs_low, grad_att, preferred_element_type=jnp.float32
    )
    grad_vals = grad_vals.astype(jnp.bfloat16)
    grad_scores = probs * (grad_probs - jnp.sum(probs * grad_probs, -1, keepdims=True))
    grad_scores = grad_scores.astype(jnp.bfloat16)
    grad_rel = jnp.sum(grad_scores, axis=0, dtype=jnp.float32)
    grad_table = jnp.einsum("ijr,hij->rh", onehot, grad_rel, precision=lax.Precision.HIGHEST)
    grad_qs = (
        jnp.einsum("whij,wjhd->wihd", grad_scores, win_k, preferred_element_type=jnp.float32)
        * scale_qk
    )
    grad_ks = (
        jnp.einsum("whij,wihd->wjhd", grad_scores, win_q, preferred_element_type=jnp.float32)
        * scale_qk
    )
    stacked = jnp.stack([grad_qs.astype(jnp.bfloat16), grad_ks.astype(jnp.bfloat16), grad_vals], 2)
    stacked = stacked.reshape(win_count, WIN * WIN, 3 * channels)
    grad_proj_in = from_windows(stacked, offset, images_here)
    grad_qkv = outer_sum(normed_low, grad_proj_in)
    col_sums = jnp.sum(grad_proj_in, axis=(0, 1), dtype=jnp.float32)
    grad_qv = jnp.concatenate([col_sums[:channels], col_sums[2 * channels :]])
    grad_normed = times_trans(grad_proj_in, w_qkv)
    grad_in_norm, grad_gain_one, grad_beta_one = norm_backward(
        grad_normed, unit_one, inverse_one, norm1_gain
    )
    grad_inputs = grad_middle + grad_in_norm
    big_grads = (grad_qkv, grad_proj, grad_fc1, grad_fc2)
    small_grads = (
        grad_gain_one,
        grad_beta_one,
        grad_qv,
        grad_table,
        grad_proj_bias,
        grad_gain_two,
        grad_beta_two,
        grad_fc1_bias,
        grad_fc2_bias,
    )
    return (grad_inputs, big_grads, small_grads)


def add_trees(total, extra):
    if total is None:
        return extra
    return jax.tree.map(jnp.add, total, extra)


def shards(
    images,
    cotangent,
    region,
    rel_index,
    norm1_gain,
    norm1_bias,
    w_qkv,
    qv_bias,
    rel_table,
    w_proj,
    proj_bias,
    norm2_gain,
    norm2_bias,
    w_fc1,
    fc1_bias,
    w_fc2,
    fc2_bias,
):
    section_id = lax.axis_index("section")
    offset = section_id * SHIFT
    masked_on = section_id.astype(jnp.float32)
    micro = images.shape[0]
    table_rows = rel_table.shape[1]
    onehot = (
        rel_index[:, :, None] == jnp.arange(table_rows, dtype=jnp.int32)[None, None, :]
    ).astype(jnp.float32)
    rel_bias = jnp.einsum("ijr,rh->hij", onehot, rel_table[0], precision=lax.Precision.HIGHEST)
    labels = to_windows(region.reshape(1, -1, 1), 0)[..., 0]
    mask_add = (
        jnp.where(labels[:, :, None] == labels[:, None, :], 0.0, -100.0).astype(jnp.float32)
        * masked_on
    )
    small = (
        norm1_gain[0],
        norm1_bias[0],
        qv_bias[0],
        proj_bias[0],
        norm2_gain[0],
        norm2_bias[0],
        fc1_bias[0],
        fc2_bias[0],
    )

    def fetch_weights():
        return (
            lax.all_gather(w_qkv[0], "shard", axis=0, tiled=True),
            lax.all_gather(w_proj[0], "shard", axis=0, tiled=True),
            lax.all_gather(w_fc1[0], "shard", axis=0, tiled=True),
            lax.all_gather(w_fc2[0], "shard", axis=0, tiled=True),
        )

    received = jnp.zeros(images.shape[1:], jnp.bfloat16)
    inputs_kept = []
    outputs_kept = []
    for turn_no in range(micro + 1):
        mats = fetch_weights()
        entering = jnp.where(section_id == 0, images[min(turn_no, micro - 1)], received)
        output, saved = layer_forward(
            entering.astype(jnp.float32), small, mats, offset, mask_add, rel_bias
        )
        output_low = output.astype(jnp.bfloat16)
        inputs_kept.append(entering)
        outputs_kept.append(output_low)
        if turn_no < micro:
            received = shifted(output_low, "section", 1)
    own_inputs = lax.dynamic_slice_in_dim(jnp.stack(inputs_kept), section_id, micro, 0)
    section_out = lax.dynamic_slice_in_dim(jnp.stack(outputs_kept), section_id, micro, 0)[None]
    coming_back = jnp.zeros(images.shape[1:], jnp.bfloat16)
    grads_kept = []
    big_total = None
    small_total = None
    owned = None
    for turn_no in range(micro + 1):
        mats = fetch_weights()
        which_mb = turn_no - 1 + section_id
        useful = ((which_mb >= 0) & (which_mb < micro)).astype(jnp.float32)
        clamped = jnp.clip(which_mb, 0, micro - 1)
        layer_in = lax.dynamic_index_in_dim(own_inputs, clamped, 0, keepdims=False).astype(
            jnp.float32
        )
        incoming = jnp.where(section_id == 1, cotangent[min(turn_no, micro - 1)], coming_back)
        incoming = incoming.astype(jnp.float32) * useful
        grad_inputs, big_grads, small_grads = layer_backward(
            layer_in, incoming, small, mats, offset, mask_add, rel_bias, onehot
        )
        grads_kept.append(grad_inputs)
        if turn_no < micro:
            coming_back = shifted(grad_inputs.astype(jnp.bfloat16), "section", -1)
        small_total = add_trees(small_total, small_grads)
        big_total = add_trees(big_total, big_grads)
    owned = jax.tree.map(
        lambda part: part.astype(jnp.float32),
        lax.psum_scatter(shortened(big_total), "shard", scatter_dimension=0, tiled=True),
    )
    input_grad = lax.dynamic_slice_in_dim(jnp.stack(grads_kept), 1 - section_id, micro, 0)[None]
    rows_qkv, rows_proj, rows_fc1, rows_fc2 = jax.tree.map(
        lambda part: part.astype(jnp.float32), lax.psum(shortened(owned), "rep")
    )
    gain_one, beta_one, qv_sum, table_sum, proj_sum, gain_two, beta_two, fc1_sum, fc2_sum = (
        lax.psum(small_total, ("shard", "rep"))
    )
    return (
        section_out,
        input_grad,
        gain_one[None],
        beta_one[None],
        rows_qkv[None],
        qv_sum[None],
        table_sum[None],
        rows_proj[None],
        proj_sum[None],
        gain_two[None],
        beta_two[None],
        rows_fc1[None],
        fc1_sum[None],
        rows_fc2[None],
        fc2_sum[None],
    )


def solution(mesh):
    placed = (
        P(None, ("shard", "rep"), None, None),
        P(None, ("shard", "rep"), None, None),
        P(),
        P(),
        P("section", None),
        P("section", None),
        P("section", "shard", None),
        P("section", None),
        P("section", None, None),
        P("section", "shard", None),
        P("section", None),
        P("section", None),
        P("section", None),
        P("section", "shard", None),
        P("section", None),
        P("section", "shard", None),
        P("section", None),
    )
    return jax.shard_map(
        shards,
        mesh=mesh,
        in_specs=placed,
        out_specs=(
            P("section", None, ("shard", "rep"), None, None),
            P("section", None, ("shard", "rep"), None, None),
            P("section", None),
            P("section", None),
            P("section", "shard", None),
            P("section", None),
            P("section", None, None),
            P("section", "shard", None),
            P("section", None),
            P("section", None),
            P("section", None),
            P("section", "shard", None),
            P("section", None),
            P("section", "shard", None),
            P("section", None),
        ),
        check_vma=False,
    )
```

profile of v0, /device:TPU:0, one launch (start us, length us, event | category | flops | bytes accessed | tf_op | source)
XLA Modules:
  0.0 1423.8 jit_solution(8498349651648289992)
XLA Ops:
  9.5 21.4 %all-gather.1 = bf16[1,512,512]{2,1,0:T(8,128)(2,1)S(1)} all-gather(bf16[1,128,512]{2,1,0:T(8,128)(2,1)} %param.30), channel_id=3, replica_groups=mesh['section'=2,'shard'=4,'rep'=4] {'shard'}, dimensions={1}, use_global_device_ids=true | all-gather | bytes 655360 | tf_op jit(solution)/shard_map/all_gather | solution.py:295
  38.2 13.5 all-gather.8.cloned.1.call-done
  109.3 36.0 %all-gather.12.cloned.1.call-done = bf16[1,2048,512]{2,1,0:T(8,128)(2,1)} async-done(((bf16[1,512,512]{2,1,0:T(8,128)(2,1)}), bf16[1,2048,512]{2,1,0:T(8,128)(2,1)}) %all-gather.12.cloned.1.call-update) | async-done | bytes 2097168 | tf_op jit(solution)/shard_map/all_gather | solution.py:297
  145.3 11.3 bitcast_dynamic-update-slice_fusion.11
  170.3 7.4 reshape_reshape.138
  218.6 9.3 bitcast_dynamic-update-slice_fusion.10
  241.9 7.4 reshape_reshape.140
  290.1 9.2 bitcast_dynamic-update-slice_fusion.9
  361.5 9.3 bitcast_dynamic-update-slice_fusion.8
  389.2 7.3 reshape_reshape.146
  471.6 10.0 copy.296
  481.5 7.8 reshape_reshape.149
  568.6 7.5 reshape_reshape.144
  622.2 11.9 fusion.277
  689.7 10.0 copy.316
  699.7 8.2 reshape_reshape.153
  730.7 7.3 reshape_reshape.154
  850.1 7.5 reshape_reshape.158
  907.0 10.1 fusion.275
  995.9 10.0 copy.336
  1005.8 8.0 reshape_reshape.157
  1079.9 10.0 copy.356
  1089.8 7.9 reshape_reshape.161
  1156.5 10.0 copy.375
  1166.4 8.2 reshape_reshape.165
  1198.1 11.5 fusion.273
  1217.5 10.3 fusion.271
  1227.9 9.9 fusion.10
  1238.2 10.5 fusion.431
  1264.0 23.3 %reduce-scatter.9.cloned.1.call-done = bf16[128,2048]{1,0:T(8,128)(2,1)} async-done(((bf16[512,2048]{1,0:T(8,128)(2,1)}), bf16[128,2048]{1,0:T(8,128)(2,1)}) %reduce-scatter.9.cloned.1.call-update) | async-done | bytes 524304 | tf_op jit(solution)/shard_map/reduce_scatter | solution.py:341
  1287.3 45.6 %reduce-scatter.11.cloned.1.call-done = bf16[512,512]{1,0:T(8,128)(2,1)} async-done(((bf16[2048,512]{1,0:T(8,128)(2,1)}), bf16[512,512]{1,0:T(8,128)(2,1)}) %reduce-scatter.11.cloned.1.call-update) | async-done | bytes 524304 | tf_op jit(solution)/shard_map/reduce_scatter | solution.py:341
  1333.4 76.2 %all-reduce = (f32[1,512]{1,0:T(1,128)}, f32[1,512]{1,0:T(1,128)}, f32[1,1024]{1,0:T(1,128)}, f32[1,169,16]{1,2,0:T(8,128)}, f32[1,512]{1,0:T(1,128)}, /*index=5...) all-reduce(f32[1,512]{1,0:T(1,128)S(1)} %bitcast.1457, ...), channel_id=1, replica_groups=mesh['section'=2,'shard'=4,'rep'=4] {'shard','rep'}, use_global_device_ids=true, to_apply=%region_90.93 | all-reduce | flops 8848 | bytes 70784 | tf_op jit(solution)/shard_map/psum | solution.py:348
  (994 shorter events, 951.6 us)
Async XLA Ops:
  7.2 44.4 %all-gather.8.cloned.1.call-start = ((), (), s32[]{:S(2)}) async-start(), calls=%async_computation.8 | async-start | bytes 1966080 | tf_op jit(solution)/shard_map/all_gather | solution.py:294
  8.0 96.0 %all-gather.10.cloned.1.call-start = ((), (), s32[]{:S(2)}) async-start(), calls=%async_computation.9 | async-start | bytes 2621440 | tf_op jit(solution)/shard_map/all_gather | solution.py:296
  8.7 136.6 %all-gather.12.cloned.1.call-start = ((), (), s32[]{:S(2)}) async-start(), calls=%async_computation.10 | async-start | bytes 2621440 | tf_op jit(solution)/shard_map/all_gather | solution.py:297
  9.4 1254.5 %reduce-scatter.7.cloned.1.call-start = ((), (), s32[]{:S(2)}) async-start(), calls=%async_computation.5 | async-start | bytes 655360 | tf_op jit(solution)/shard_map/reduce_scatter | solution.py:341
  38.2 462.9 %copy-start.150 = (f32[1536]{0:T(1024)}, f32[1536]{0:T(1024)S(1)}, u32[]{:S(2)}) copy-start(f32[1536]{0:T(1024)S(1)} %pad_maximum_fusion.5) | copy-start | bytes 18436
  156.6 3.2 collective-permute-start
  227.8 3.6 collective-permute-start.1
  299.3 3.6 collective-permute-start.2
  370.8 7.0 collective-permute-start.3
  501.0 285.6 %copy-start.138 = (f32[2,196]{1,0:T(2,128)}, f32[2,196]{1,0:T(2,128)S(1)}, u32[]{:S(2)}) copy-start(f32[2,196]{1,0:T(2,128)S(1)} %broadcast_multiply_fusion.5) | copy-start | bytes 4708
  555.4 227.7 %copy-start.7 = (f32[2,196,512]{2,1,0:T(8,128)}, f32[2,196,512]{2,1,0:T(8,128)S(1)}, u32[]{:S(2)}) copy-start(f32[2,196,512]{2,1,0:T(8,128)S(1)} %get-tuple-element.286) | copy-start | bytes 2408452
  556.8 96.3 %collective-permute-start.4 = (bf16[2,196,512]{2,1,0:T(8,128)(2,1)}, bf16[2,196,512]{2,1,0:T(8,128)(2,1)}, u32[]{:S(2)}, u32[]{:S(2)}) collective-permute-start(bf16[2,196,512]{2,1,0:T(8,128)(2,1)} %fusion.1322), channel_id=1, source_target_pairs={{16,0},{17,1},{18,2},{19,3},{20,4},{21,5},{22,6},{23,7},{24,8},{25... | collective-permute-start | bytes 1204232 | tf_op jit(solution)/shard_map/ppermute | solution.py:17
  784.9 174.0 %collective-permute-start.5 = (bf16[2,196,512]{2,1,0:T(8,128)(2,1)}, bf16[2,196,512]{2,1,0:T(8,128)(2,1)}, u32[]{:S(2)}, u32[]{:S(2)}) collective-permute-start(bf16[2,196,512]{2,1,0:T(8,128)(2,1)} %get-tuple-element.172), channel_id=1, source_target_pairs={{16,0},{17,1},{18,2},{19,3},{20,4},{21,5},{22,6},{23,7},{24,8},{25... | collective-permute-start | bytes 1204232 | tf_op jit(solution)/shard_map/ppermute | solution.py:17
  1027.4 15.6 %collective-permute-start.6 = (bf16[2,196,512]{2,1,0:T(8,128)(2,1)}, bf16[2,196,512]{2,1,0:T(8,128)(2,1)}, u32[]{:S(2)}, u32[]{:S(2)}) collective-permute-start(bf16[2,196,512]{2,1,0:T(8,128)(2,1)} %get-tuple-element.170), channel_id=1, source_target_pairs={{16,0},{17,1},{18,2},{19,3},{20,4},{21,5},{22,6},{23,7},{24,8},{25... | collective-permute-start | bytes 1204232 | tf_op jit(solution)/shard_map/ppermute | solution.py:17
  1111.4 13.6 collective-permute-start.7
  1185.4 78.6 %reduce-scatter.5.cloned.1.call-start = ((), (), s32[]{:S(2)}) async-start(), calls=%async_computation.4 | async-start | bytes 1966080 | tf_op jit(solution)/shard_map/reduce_scatter | solution.py:341
  1198.0 89.4 %reduce-scatter.9.cloned.1.call-start = ((), (), s32[]{:S(2)}) async-start(), calls=%async_computation.6 | async-start | bytes 2621440 | tf_op jit(solution)/shard_map/reduce_scatter | solution.py:341
  1217.3 115.7 %reduce-scatter.11.cloned.1.call-start = ((), (), s32[]{:S(2)}) async-start(), calls=%async_computation.7 | async-start | bytes 2621440 | tf_op jit(solution)/shard_map/reduce_scatter | solution.py:341
  1237.8 171.8 %all-reduce.4.cloned.1.call-start = ((), (), s32[]{:S(2)}) async-start(), calls=%async_computation.11 | async-start | bytes 3145728 | tf_op jit(solution)/shard_map/psum | solution.py:345
  1262.4 70.8 %copy-start.168 = (f32[512]{0:T(512)S(1)}, f32[512]{0:T(512)}, u32[]{:S(2)}) copy-start(f32[512]{0:T(512)} %get-tuple-element.107) | copy-start | bytes 6148
  1262.4 70.8 %copy-start.172 = (f32[512]{0:T(512)S(1)}, f32[512]{0:T(512)}, u32[]{:S(2)}) copy-start(f32[512]{0:T(512)} %get-tuple-element.106) | copy-start | bytes 6148
  1262.4 70.8 %copy-start.176 = (f32[512]{0:T(512)S(1)}, f32[512]{0:T(512)}, u32[]{:S(2)}) copy-start(f32[512]{0:T(512)} %get-tuple-element.108) | copy-start | bytes 6148
  1262.5 70.8 %copy-start.146 = (f32[512]{0:T(512)S(1)}, f32[512]{0:T(512)}, u32[]{:S(2)}) copy-start(f32[512]{0:T(512)} %get-tuple-element.129) | copy-start | bytes 6148
  1262.5 70.8 %copy-start.147 = (f32[512]{0:T(512)S(1)}, f32[512]{0:T(512)}, u32[]{:S(2)}) copy-start(f32[512]{0:T(512)} %get-tuple-element.131) | copy-start | bytes 6148
  1262.5 70.8 %copy-start.148 = (f32[512]{0:T(512)S(1)}, f32[512]{0:T(512)}, u32[]{:S(2)}) copy-start(f32[512]{0:T(512)} %get-tuple-element.133) | copy-start | bytes 6148
  1262.5 70.8 %copy-start.149 = (f32[512]{0:T(512)S(1)}, f32[512]{0:T(512)}, u32[]{:S(2)}) copy-start(f32[512]{0:T(512)} %get-tuple-element.135) | copy-start | bytes 6148
  1262.5 70.8 %copy-start.157 = (f32[512]{0:T(512)S(1)}, f32[512]{0:T(512)}, u32[]{:S(2)}) copy-start(f32[512]{0:T(512)} %get-tuple-element.229) | copy-start | bytes 6148
  1262.5 70.8 %copy-start.153 = (f32[2048]{0:T(1024)S(1)}, f32[2048]{0:T(1024)}, u32[]{:S(2)}) copy-start(f32[2048]{0:T(1024)} %get-tuple-element.321) | copy-start | bytes 24580
  1262.5 70.8 %copy-start.154 = (f32[2048]{0:T(1024)S(1)}, f32[2048]{0:T(1024)}, u32[]{:S(2)}) copy-start(f32[2048]{0:T(1024)} %get-tuple-element.323) | copy-start | bytes 24580
  1262.5 70.8 %copy-start.155 = (f32[2048]{0:T(1024)S(1)}, f32[2048]{0:T(1024)}, u32[]{:S(2)}) copy-start(f32[2048]{0:T(1024)} %get-tuple-element.319) | copy-start | bytes 24580
  1262.5 70.8 %copy-start.156 = (f32[2048]{0:T(1024)S(1)}, f32[2048]{0:T(1024)}, u32[]{:S(2)}) copy-start(f32[2048]{0:T(1024)} %get-tuple-element.317) | copy-start | bytes 24580
  1333.0 83.5 %copy-start.1 = (f32[1,169,16]{1,2,0:T(8,128)S(1)}, f32[1,169,16]{1,2,0:T(8,128)}, u32[]{:S(2)}) copy-start(f32[1,169,16]{1,2,0:T(8,128)} %param.29) | copy-start | bytes 32452
  (229 other events, 2475.7 us)
Sparse Core Ops, SparseCore 0:
  9.6 41.9 all-gather.7
  53.2 45.7 all-gather.9
  100.6 44.6 all-gather.11
  1185.5 21.0 reduce-scatter.6
  1208.8 33.5 reduce-scatter.4
  1244.5 42.8 reduce-scatter.8
  1289.7 43.1 reduce-scatter.10
  1336.3 61.7 all-reduce.3
where the time goes:
time: 1440 us; the launch traced here: 1420 us
  local copies, waits for them, and re-layouts  581 us (40%)
  matrix products  390 us (27%)
  other arithmetic  195 us (14%)
  waiting for transfers between devices  124 us (9%)
  blocking collectives  97.6 us (7%)
  between operations  18.4 us (1%)
  starting transfers between devices  16.8 us (1%)
    unnamed x525, local copies, waits for them, and re-layouts  130 us
    dot_general x35, matrix products, times_plain(): jnp.dot(flat_rows(left), matrix, preferred_element_type=jnp.float32)  105 us
    dot_general x20, matrix products, outer_sum(): lax.dot_general(flat_rows(left), flat_rows(right), (((0,), (0,)), ((), ()...  101 us
    psum x1, blocking collectives, shards(): lax.psum(small_total, ('shard', 'rep'))  76.2 us
    another operation x10, local copies, waits for them, and re-layouts, layer_forward(): split_up = windowed.reshape(win_count, WIN * WIN, 3, heads_all, HEAD)  73.5 us
    another operation x15, local copies, waits for them, and re-layouts, from_windows(): tensor.reshape(images_here, per_side, per_side, WIN, WIN, channels)  72.5 us
    concatenate x30, other arithmetic, to_windows(): lattice = jnp.roll(lattice, (-offset, -offset), (1, 2))  70.6 us
    reduce_scatter x4, waiting for transfers between devices, shards(): lax.psum_scatter(shortened(big_total), 'shard', scatter_dimension=0, tile...  69 us
  transfers between devices with their start and end apart: 16, of which 7 were waited for; matrix products, arithmetic and copies ran while one was open for 31% of the time, Pallas kernels for 0%

commit v1 on v0

v1 whole, which is shorter than its diff:
```python
import functools
import math

import jax
import jax.numpy as jnp
import numpy as np
from jax import lax
from jax.experimental import pallas as pl
from jax.experimental.pallas import tpu as pltpu
from jax.sharding import PartitionSpec as P

HEAD = 32
WIN = 7
GRID = 14
SHIFT = 3
ROWS = 256
SLOT = 64
PAIR = 128
CHUNK = 512
FAR = -1e30
SCALE = 1.0 / math.sqrt(HEAD)


def mm(left, right):
    return jnp.dot(left, right, preferred_element_type=jnp.float32)


def mm_t(left, right):
    return lax.dot_general(
        left, right, (((1,), (1,)), ((), ())), preferred_element_type=jnp.float32
    )


def mm_outer(left, right):
    return lax.dot_general(
        left, right, (((0,), (0,)), ((), ())), preferred_element_type=jnp.float32
    )


def unit(values):
    centred = values - jnp.mean(values, -1, keepdims=True)
    inverse = lax.rsqrt(jnp.mean(centred * centred, -1, keepdims=True) + 1e-05)
    return centred * inverse, inverse


def unit_back(grad, unit_rows, inverse, gain):
    scaled = grad * gain
    return inverse * (
        scaled
        - jnp.mean(scaled, -1, keepdims=True)
        - unit_rows * jnp.mean(scaled * unit_rows, -1, keepdims=True)
    )


def col(values):
    return jnp.sum(values, axis=0, keepdims=True)


def layer_kernel(backward, *refs):
    if backward:
        (x_ref, cot_ref, perm, back, wqkv, bqkv, wproj, vecs, w1, b1, w2, bias, hm,
         out_ref, dx_ref, gqkv_o, gproj_o, g1_o, g2_o, gvec, gcol, gfc1b, drel,
         x_s, a_s, qkv_s, att_s, b_s, acc_s, probs_s, u1_s, u2_s,
         dy_s, db_s, dqkv_s, datt_s, gqkv, gproj, g1, g2) = refs
        for ref in (gvec, gcol, gfc1b, drel, gqkv, gproj, g1, g2):
            ref[...] = jnp.zeros_like(ref)
    else:
        (x_ref, perm, back, wqkv, bqkv, wproj, vecs, w1, b1, w2, bias, hm, out_ref,
         x_s, a_s, qkv_s, att_s, b_s, acc_s) = refs
    channels = wproj.shape[0]
    groups = channels // PAIR
    steps = (ROWS // PAIR) * groups
    heads = PAIR // HEAD

    def place(t):
        rows = pl.ds(pl.multiple_of((t // groups) * PAIR, PAIR), PAIR)
        g = t % groups

        def lanes(which):
            return pl.ds(pl.multiple_of(which * channels + g * PAIR, PAIR), PAIR)

        return rows, g, lanes

    def spread(block):
        return jnp.concatenate([block] * heads, axis=0) * hm[...]

    def gathered(stack):
        total = stack[:PAIR] * hm[:PAIR].astype(jnp.float32)
        for h in range(1, heads):
            part = slice(h * PAIR, (h + 1) * PAIR)
            total = total + stack[part] * hm[part].astype(jnp.float32)
        return total

    def one_image(i, carry):
        x = mm(perm[...], x_ref[i])
        x_s[...] = x
        unit_one, inv_one = unit(x)
        a_s[...] = (unit_one * vecs[0:1] + vecs[1:2]).astype(jnp.bfloat16)
        if backward:
            u1_s[...] = unit_one
        for part in range(3):
            cols = slice(part * channels, (part + 1) * channels)
            qkv_s[:, cols] = (mm(a_s[...], wqkv[:, cols]) + bqkv[:, cols]).astype(jnp.bfloat16)

        def attend(t, c):
            rows, g, lanes = place(t)
            scores = mm_t(qkv_s[rows, lanes(0)], spread(qkv_s[rows, lanes(1)]))
            scores = scores * SCALE + bias[t]
            parts = []
            for h in range(heads):
                s = scores[:, h * PAIR:(h + 1) * PAIR]
                e = jnp.exp(s - jnp.max(s, -1, keepdims=True))
                parts.append(e * (1.0 / jnp.sum(e, -1, keepdims=True)))
            probs = jnp.concatenate(parts, axis=1)
            if backward:
                probs_s[t] = probs
            att_s[rows, lanes(0)] = mm(
                probs.astype(jnp.bfloat16), spread(qkv_s[rows, lanes(2)])
            ).astype(jnp.bfloat16)
            return c

        lax.fori_loop(0, steps, attend, 0)
        middle = x_s[...] + (mm(att_s[...], wproj[...]) + vecs[2:3])
        x_s[...] = middle
        unit_two, inv_two = unit(middle)
        b_s[...] = (unit_two * vecs[3:4] + vecs[4:5]).astype(jnp.bfloat16)
        acc_s[...] = jnp.zeros_like(acc_s)
        if backward:
            u2_s[...] = unit_two
            dy_s[...] = mm(perm[...], cot_ref[i]).astype(jnp.bfloat16)
            db_s[...] = jnp.zeros_like(db_s)

        def ffn(c, k):
            cols = pl.ds(pl.multiple_of(c * CHUNK, CHUNK), CHUNK)
            hidden = mm(b_s[...], w1[:, cols]) + b1[:, cols]
            cdf = 0.5 * (1.0 + lax.erf(hidden * (1.0 / math.sqrt(2.0))))
            act = (hidden * cdf).astype(jnp.bfloat16)
            acc_s[...] += mm(act, w2[cols, :])
            if backward:
                pdf = jnp.exp(-0.5 * hidden * hidden) * (1.0 / math.sqrt(2.0 * math.pi))
                dact = mm_t(dy_s[...], w2[cols, :])
                dhid_f = dact * (cdf + hidden * pdf)
                dhid = dhid_f.astype(jnp.bfloat16)
                g2[cols, :] += mm_outer(act, dy_s[...])
                g1[:, cols] += mm_outer(b_s[...], dhid)
                gfc1b[:, cols] += col(dhid.astype(jnp.float32))
                db_s[...] += mm_t(dhid, w1[:, cols])
            return k

        lax.fori_loop(0, w1.shape[1] // CHUNK, ffn, 0)
        out = (x_s[...] + (acc_s[...] + vecs[5:6])).astype(jnp.bfloat16)
        out_ref[i] = mm(back[...], out).astype(jnp.bfloat16)
        if not backward:
            return carry
        db = db_s[...]
        gvec[3:4] += col(db * u2_s[...])
        gvec[4:5] += col(db)
        dy = dy_s[...].astype(jnp.float32)
        gvec[5:6] += col(dy)
        dmid = dy + unit_back(db, u2_s[...], inv_two, vecs[3:4])
        x_s[...] = dmid
        dz = dmid.astype(jnp.bfloat16)
        gvec[2:3] += col(dz.astype(jnp.float32))
        gproj[...] += mm_outer(att_s[...], dz)
        datt_s[...] = mm_t(dz, wproj[...]).astype(jnp.bfloat16)

        def attend_back(t, c):
            rows, g, lanes = place(t)
            datt = datt_s[rows, lanes(0)]
            probs = probs_s[t]
            dprobs = mm_t(datt, spread(qkv_s[rows, lanes(2)]))
            dqkv_s[rows, lanes(2)] = gathered(
                mm_outer(probs.astype(jnp.bfloat16), datt)
            ).astype(jnp.bfloat16)
            parts = []
            for h in range(heads):
                here = slice(h * PAIR, (h + 1) * PAIR)
                p = probs[:, here]
                d = dprobs[:, here]
                parts.append(p * (d - jnp.sum(p * d, -1, keepdims=True)))
            dscores = jnp.concatenate(parts, axis=1).astype(jnp.bfloat16)
            drel[g] += dscores.astype(jnp.float32)
            dqkv_s[rows, lanes(0)] = (
                mm(dscores, spread(qkv_s[rows, lanes(1)])) * SCALE
            ).astype(jnp.bfloat16)
            dqkv_s[rows, lanes(1)] = (
                gathered(mm_outer(dscores, qkv_s[rows, lanes(0)])) * SCALE
            ).astype(jnp.bfloat16)
            return c

        lax.fori_loop(0, steps, attend_back, 0)
        for part in range(3):
            cols = slice(part * channels, (part + 1) * channels)
            gqkv[:, cols] += mm_outer(a_s[...], dqkv_s[:, cols])
            gcol[:, cols] += col(dqkv_s[:, cols].astype(jnp.float32))
        da = mm_t(dqkv_s[...], wqkv[...])
        gvec[0:1] += col(da * u1_s[...])
        gvec[1:2] += col(da)
        dx = x_s[...] + unit_back(da, u1_s[...], inv_one, vecs[0:1])
        high = dx.astype(jnp.bfloat16)
        rest = (dx - high.astype(jnp.float32)).astype(jnp.bfloat16)
        dx_ref[i] = mm(back[...], high) + mm(back[...], rest)
        return carry

    lax.fori_loop(0, x_ref.shape[0], one_image, 0)
    if backward:
        gqkv_o[...] = gqkv[...].astype(jnp.bfloat16)
        gproj_o[...] = gproj[...].astype(jnp.bfloat16)
        g1_o[...] = g1[...].astype(jnp.bfloat16)
        g2_o[...] = g2[...].astype(jnp.bfloat16)


def call_layer(x, cot, consts, mats, small):
    perm, back, hm = consts
    wqkv, wproj, w1, w2 = mats
    bqkv, vecs, b1, bias = small
    backward = cot is not None
    n = x.shape[0]
    c, f = w1.shape
    low, full = jnp.bfloat16, jnp.float32
    t = bias.shape[0]
    tokens = (ROWS, c)
    heads = PAIR // HEAD
    outs = [jax.ShapeDtypeStruct((n,) + tokens, low)]
    scratch = [
        pltpu.VMEM(tokens, full),
        pltpu.VMEM(tokens, low),
        pltpu.VMEM((ROWS, 3 * c), low),
        pltpu.VMEM(tokens, low),
        pltpu.VMEM(tokens, low),
        pltpu.VMEM(tokens, full),
    ]
    if backward:
        outs += [
            jax.ShapeDtypeStruct((n,) + tokens, full),
            jax.ShapeDtypeStruct(wqkv.shape, low),
            jax.ShapeDtypeStruct(wproj.shape, low),
            jax.ShapeDtypeStruct(w1.shape, low),
            jax.ShapeDtypeStruct(w2.shape, low),
            jax.ShapeDtypeStruct((8, c), full),
            jax.ShapeDtypeStruct((1, 3 * c), full),
            jax.ShapeDtypeStruct((1, f), full),
            jax.ShapeDtypeStruct((c // PAIR, PAIR, heads * PAIR), full),
        ]
        scratch += [
            pltpu.VMEM((t, PAIR, heads * PAIR), full),
            pltpu.VMEM(tokens, full),
            pltpu.VMEM(tokens, full),
            pltpu.VMEM(tokens, low),
            pltpu.VMEM(tokens, full),
            pltpu.VMEM((ROWS, 3 * c), low),
            pltpu.VMEM(tokens, low),
            pltpu.VMEM(wqkv.shape, full),
            pltpu.VMEM(wproj.shape, full),
            pltpu.VMEM(w1.shape, full),
            pltpu.VMEM(w2.shape, full),
        ]
    args = (x,) + ((cot,) if backward else ())
    args += (perm, back, wqkv, bqkv, wproj, vecs, w1, b1, w2, bias, hm)
    vmem = pl.BlockSpec(memory_space=pltpu.VMEM)
    return pl.pallas_call(
        functools.partial(layer_kernel, backward),
        out_shape=outs,
        in_specs=[vmem] * len(args),
        out_specs=[vmem] * len(outs),
        scratch_shapes=scratch,
        compiler_params=pltpu.CompilerParams(vmem_limit_bytes=58 * 2**20),
        cost_estimate=pl.CostEstimate(
            flops=2 * n * ROWS * c * (4 * c + 2 * f) * (3 if backward else 1),
            bytes_accessed=2 * c * (4 * c + 2 * f),
            transcendentals=n * ROWS * f,
        ),
    )(*args)


def window_order(offset):
    matrix = np.zeros((ROWS, ROWS), np.float32)
    side = GRID // WIN
    for w in range(side * side):
        for i in range(WIN * WIN):
            row = (w // side) * WIN + i // WIN
            column = (w % side) * WIN + i % WIN
            token = ((row + offset) % GRID) * GRID + (column + offset) % GRID
            matrix[w * SLOT + i, token] = 1.0
    return matrix


def window_bias(rel, mask):
    heads = rel.shape[0]
    count = mask.shape[0]
    area = WIN * WIN
    more = SLOT - area
    block = rel[None] + mask[:, None]
    block = jnp.pad(block, ((0, 0), (0, 0), (0, more), (0, 0)))
    block = jnp.pad(block, ((0, 0), (0, 0), (0, 0), (0, more)), constant_values=FAR)
    block = block.reshape(count // 2, 2, heads, SLOT, SLOT)
    first = jnp.pad(block[:, 0], ((0, 0), (0, 0), (0, 0), (0, SLOT)), constant_values=FAR)
    second = jnp.pad(block[:, 1], ((0, 0), (0, 0), (0, 0), (SLOT, 0)), constant_values=FAR)
    both = jnp.concatenate([first, second], axis=2)
    per = PAIR // HEAD
    both = both.reshape(count // 2, heads // per, per, PAIR, PAIR).transpose(0, 1, 3, 2, 4)
    return both.reshape(count // 2 * (heads // per), PAIR, per * PAIR)


def table_grad(drel, onehot):
    groups = drel.shape[0]
    area = WIN * WIN
    split = drel.reshape(groups, 2, SLOT, PAIR // HEAD, 2, SLOT)
    total = split[:, 0, :area, :, 0, :area] + split[:, 1, :area, :, 1, :area]
    return jnp.einsum("ijr,gihj->rgh", onehot, total, precision=lax.Precision.HIGHEST).reshape(
        onehot.shape[-1], -1
    )


def to_windows(tensor):
    side = GRID // WIN
    lattice = tensor.reshape(side, WIN, side, WIN).transpose(0, 2, 1, 3)
    return lattice.reshape(side * side, WIN * WIN)


def shards(
    images,
    cotangent,
    region,
    rel_index,
    norm1_gain,
    norm1_bias,
    w_qkv,
    qv_bias,
    rel_table,
    w_proj,
    proj_bias,
    norm2_gain,
    norm2_bias,
    w_fc1,
    fc1_bias,
    w_fc2,
    fc2_bias,
):
    section_id = lax.axis_index("section")
    first = section_id == 0
    micro, per, tokens, channels = images.shape
    half = micro // 2
    table_rows = rel_table.shape[1]
    heads = rel_table.shape[2]
    hidden = fc1_bias.shape[1]
    own_mats = tuple(
        lax.all_gather(part[0], "shard", axis=0, tiled=True)
        for part in (w_qkv, w_proj, w_fc1, w_fc2)
    )
    from_zero = [(0, 1)]
    from_one = [(1, 0)]

    def moved(tree, route):
        return jax.tree.map(lambda part: lax.ppermute(part, "section", route), tree)

    def choose(on_zero, on_one):
        return jax.tree.map(lambda l, r: jnp.where(first, l, r), on_zero, on_one)

    mats_zero = choose(own_mats, moved(own_mats, from_zero))
    mats_one = choose(moved(own_mats, from_one), own_mats)
    small_list = (
        norm1_gain, norm1_bias, proj_bias, norm2_gain, norm2_bias, fc2_bias, qv_bias, fc1_bias,
        rel_table,
    )
    small_flat = jnp.concatenate([part.reshape(-1) for part in small_list])
    small_both = lax.all_gather(small_flat, "section", axis=0)
    onehot = (
        rel_index[:, :, None] == jnp.arange(table_rows, dtype=jnp.int32)[None, None, :]
    ).astype(jnp.float32)
    labels = to_windows(region)
    region_mask = jnp.where(labels[:, :, None] == labels[:, None, :], 0.0, -100.0).astype(
        jnp.float32
    )

    def small_of(layer):
        flat = small_both[layer]
        six = flat[: 6 * channels].reshape(6, channels)
        vecs = jnp.pad(six, ((0, 2), (0, 0)))
        at = 6 * channels
        qv = flat[at:at + 2 * channels]
        at += 2 * channels
        b1 = flat[at:at + hidden]
        at += hidden
        table = flat[at:].reshape(table_rows, heads)
        bqkv = jnp.concatenate([qv[:channels], jnp.zeros((channels,), jnp.float32), qv[channels:]])
        rel = jnp.einsum("ijr,rh->hij", onehot, table, precision=lax.Precision.HIGHEST)
        mask = region_mask if layer == 1 else jnp.zeros_like(region_mask)
        return (bqkv[None], vecs, b1[None], window_bias(rel, mask))

    lane_head = np.arange(PAIR) // HEAD
    hm = np.zeros((PAIR // HEAD, PAIR, PAIR), np.float32)
    for h in range(PAIR // HEAD):
        hm[h] = lane_head == h
    hm = jnp.asarray(hm.reshape(-1, PAIR), jnp.bfloat16)

    def consts_of(offset):
        perm = window_order(offset)
        return jnp.asarray(perm, jnp.bfloat16), jnp.asarray(perm.T, jnp.bfloat16), hm

    def mine(array):
        part = lax.dynamic_slice_in_dim(array, section_id * half, half, 0)
        part = part.reshape(half * per, tokens, channels)
        return jnp.pad(part, ((0, 0), (0, ROWS - tokens), (0, 0)))

    def trimmed(array):
        return array[:, :tokens].reshape(half, per, tokens, channels)

    x0 = mine(images)
    cot = mine(cotangent)
    consts_zero, consts_one = consts_of(0), consts_of(SHIFT)
    small_zero, small_one = small_of(0), small_of(1)
    (x1,) = call_layer(x0, None, consts_zero, mats_zero, small_zero)
    res_one = call_layer(x1, cot, consts_one, mats_one, small_one)
    out_one, dx_one, big_one = res_one[0], res_one[1], tuple(res_one[2:6])
    sent_one = moved((trimmed(out_one), trimmed(dx_one), big_one), from_zero)
    res_zero = call_layer(x0, dx_one.astype(jnp.bfloat16), consts_zero, mats_zero, small_zero)
    dx_zero, big_zero = res_zero[1], tuple(res_zero[2:6])
    x1_there = moved(trimmed(x1), from_one)
    dx_there, big_there = moved((trimmed(dx_zero), big_zero), from_one)

    def whole(zero_own, zero_there, one_own, one_there):
        on_zero = jnp.concatenate([zero_own, zero_there], 0)
        on_one = jnp.concatenate([one_there, one_own], 0)
        return jnp.where(first, on_zero, on_one)[None]

    section_out = whole(trimmed(x1), x1_there, trimmed(out_one), sent_one[0])
    input_grad = whole(trimmed(dx_zero), dx_there, trimmed(dx_one), sent_one[1])

    def summed(zero_own, zero_there, one_own, one_there):
        own = jnp.where(first, zero_own, one_own).astype(jnp.float32)
        there = jnp.where(first, zero_there, one_there).astype(jnp.float32)
        return (own + there).astype(jnp.bfloat16)

    big_total = jax.tree.map(summed, big_zero, big_there, big_one, sent_one[2])
    owned = lax.psum_scatter(big_total, "shard", scatter_dimension=0, tiled=True)
    rows_qkv, rows_proj, rows_fc1, rows_fc2 = jax.tree.map(
        lambda part: part.astype(jnp.float32), lax.psum(owned, "rep")
    )

    def small_grads(res):
        gvec, gcol, gfc1b, drel = res[6:10]
        return jnp.concatenate(
            [
                gvec[:6].reshape(-1), gcol[0, :channels], gcol[0, 2 * channels:], gfc1b[0],
                table_grad(drel, onehot).reshape(-1),
            ]
        )

    small_sum = lax.psum(
        jnp.stack([small_grads(res_zero), small_grads(res_one)]), ("section", "shard", "rep")
    )
    flat = jnp.where(first, small_sum[0], small_sum[1])
    six = flat[: 6 * channels].reshape(6, 1, channels)
    at = 6 * channels
    qv_sum = flat[at:at + 2 * channels][None]
    at += 2 * channels
    fc1_sum = flat[at:at + hidden][None]
    table_sum = flat[at + hidden:].reshape(1, table_rows, heads)
    return (
        section_out,
        input_grad,
        six[0],
        six[1],
        rows_qkv[None],
        qv_sum,
        table_sum,
        rows_proj[None],
        six[2],
        six[3],
        six[4],
        rows_fc1[None],
        fc1_sum,
        rows_fc2[None],
        six[5],
    )


def solution(mesh):
    placed = (
        P(None, ("shard", "rep"), None, None),
        P(None, ("shard", "rep"), None, None),
        P(),
        P(),
        P("section", None),
        P("section", None),
        P("section", "shard", None),
        P("section", None),
        P("section", None, None),
        P("section", "shard", None),
        P("section", None),
        P("section", None),
        P("section", None),
        P("section", "shard", None),
        P("section", None),
        P("section", "shard", None),
        P("section", None),
    )
    return jax.shard_map(
        shards,
        mesh=mesh,
        in_specs=placed,
        out_specs=(
            P("section", None, ("shard", "rep"), None, None),
            P("section", None, ("shard", "rep"), None, None),
            P("section", None),
            P("section", None),
            P("section", "shard", None),
            P("section", None),
            P("section", None, None),
            P("section", "shard", None),
            P("section", None),
            P("section", None),
            P("section", None),
            P("section", "shard", None),
            P("section", None),
            P("section", "shard", None),
            P("section", None),
        ),
        check_vma=False,
    )
```

time: 1440 us -> 658 us (0.46)
  local copies, waits for them, and re-layouts: 581 us -> 54.5 us
  matrix products: 390 us -> 7.1 us
  Pallas kernels: 0 us -> 199 us
  other arithmetic: 195 us -> 52.2 us
  waiting for transfers between devices: 124 us -> 243 us
  blocking collectives: 97.6 us -> 21.1 us
  starting transfers between devices: 16.8 us -> 55.8 us
    dot_general x111 -> x4, matrix products: 336 us -> 7.1 us  [the longest x2 4.62 us: small_of(): jnp.einsum('ijr,rh->hij', onehot, table, precision=lax.Precision.HIGHEST)]
    another operation x51 -> x5, local copies, waits for them, and re-layouts: 255 us -> 0.71 us  [the longest x2 0.66 us: small_grads(): table_grad(drel, onehot).reshape(-1)]
    pallas_call x0 -> x3, Pallas kernels: none -> 199 us  [call_layer(): pl.pallas_call(functools.partial(layer_kernel, backward), out_shape=outs,...]
    psum x1 -> x2, waiting for transfers between devices: 0.01 us -> 168 us  [the longest x1 116 us: shards(): lax.psum(jnp.stack([small_grads(res_zero), small_grads(res_one)]), ('sect...]
    unnamed x525 -> x69, local copies, waits for them, and re-layouts: 130 us -> 12.5 us
    concatenate x54 -> x3, other arithmetic: 108 us -> 2.13 us  [the longest x2 2.12 us: window_bias(): both = jnp.concatenate([first, second], axis=2)]
    psum x1 -> x0, blocking collectives: 76.2 us -> none  [shards(): lax.psum(small_total, ('shard', 'rep'))]
    reduce_scatter x4, waiting for transfers between devices: 69 us -> 0.04 us  [shards(): lax.psum_scatter(big_total, 'shard', scatter_dimension=0, tiled=True)]
  transfers between devices with their start and end apart: 16 -> 30, of which waited for: 7 -> 10; matrix products, arithmetic and copies ran while one was open for 31% -> 13% of each run, Pallas kernels for 0% -> 0%
where the time goes in v1:
time: 658 us; the launch traced here: 650 us
  waiting for transfers between devices  243 us (37%)
  Pallas kernels  199 us (30%)
  starting transfers between devices  55.8 us (8%)
  local copies, waits for them, and re-layouts  54.5 us (8%)
  other arithmetic  52.2 us (8%)
  blocking collectives  21.1 us (3%)
  between operations  17.3 us (3%)
  matrix products  7.1 us (1%)
    pallas_call x3, Pallas kernels, call_layer(): pl.pallas_call(functools.partial(layer_kernel, backward), out_shape=outs,...  199 us
    psum x1, waiting for transfers between devices, shards(): lax.psum(jnp.stack([small_grads(res_zero), small_grads(res_one)]), ('sect...  116 us
    all_gather x3, waiting for transfers between devices, shards(): lax.all_gather(part[0], 'shard', axis=0, tiled=True)  66 us
    ppermute x20, starting transfers between devices, moved(): return jax.tree.map(lambda part: lax.ppermute(part, 'section', route), tree)  55.4 us
    psum x1, waiting for transfers between devices, shards(): lax.psum(owned, 'rep')  52.3 us
    all_gather x1, blocking collectives, shards(): lax.all_gather(part[0], 'shard', axis=0, tiled=True)  21.1 us
    convert_element_type x4, other arithmetic, summed(): return (own + there).astype(jnp.bfloat16)  13.9 us
  transfers between devices with their start and end apart: 30, of which 10 were waited for; matrix products, arithmetic and copies ran while one was open for 13% of the time, Pallas kernels for 0%

profile of v1, /device:TPU:0, one launch (start us, length us, event | category | flops | bytes accessed | tf_op | source)
XLA Modules:
  0.0 650.4 jit_solution(1691524188041085025)
XLA Ops:
  19.6 21.1 %all-gather.2 = bf16[1,512,512]{2,1,0:T(8,128)(2,1)S(1)} all-gather(bf16[1,128,512]{2,1,0:T(8,128)(2,1)} %param.31), channel_id=4, replica_groups=mesh['section'=2,'shard'=4,'rep'=4] {'shard'}, dimensions={1}, use_global_device_ids=true | all-gather | bytes 655360 | tf_op jit(solution)/shard_map/all_gather | solution.py:348
  48.1 2.3 fusion.2
  54.5 6.9 %all-gather.9.cloned.1.call-done = bf16[1,512,1536]{2,1,0:T(8,128)(2,1)} async-done(((bf16[1,128,1536]{2,1,0:T(8,128)(2,1)}), bf16[1,512,1536]{2,1,0:T(8,128)(2,1)}) %all-gather.9.cloned.1.call-update) | async-done | bytes 1572880 | tf_op jit(solution)/shard_map/all_gather | solution.py:348
  64.9 5.3 collective-permute-start
  71.9 36.4 %all-gather.11.cloned.1.call-done = bf16[1,512,2048]{2,1,0:T(8,128)(2,1)} async-done(((bf16[1,128,2048]{2,1,0:T(8,128)(2,1)}), bf16[1,512,2048]{2,1,0:T(8,128)(2,1)}) %all-gather.11.cloned.1.call-update) | async-done | bytes 2097168 | tf_op jit(solution)/shard_map/all_gather | solution.py:348
  109.6 5.7 collective-permute-start.2
  115.4 2.3 collective-permute-start.1
  119.0 4.3 copy.87
  123.4 3.1 reshape.315.refs_10_.refs_11_
  131.5 22.7 %all-gather.13.cloned.1.call-done = bf16[1,2048,512]{2,1,0:T(8,128)(2,1)} async-done(((bf16[1,512,512]{2,1,0:T(8,128)(2,1)}), bf16[1,2048,512]{2,1,0:T(8,128)(2,1)}) %all-gather.13.cloned.1.call-update) | async-done | bytes 2097168 | tf_op jit(solution)/shard_map/all_gather | solution.py:348
  155.5 3.3 collective-permute-start.3
  160.5 4.0 broadcast_select_fusion.5
  164.5 4.2 broadcast_select_fusion.3
  171.0 37.3 %shard_map.325.refs_0_ = bf16[4,256,512]{2,1,0:T(8,128)(2,1)} custom-call(bf16[4,256,512]{2,1,0:T(8,128)(2,1)} %pad.42.refs_0_, bf16[256,256]{1,0:T(8,128)(2,1)} %constant.33.clone.refs_1_.refs_2_, bf16[256,256]{1,0:T(8,128)(2,1)} %constant.34.clone.refs_2_.refs_3_, bf16[512,1536]{1,0:T(8,128)(2,1)} %get-tuple-element.104.refs_3_.refs_4_, ...), custom_call_target="tpu_custom_call" | custom-call | flops 6442450944 | bytes 6291456 | tf_op jit(solution)/shard_map/pallas_call | solution.py:261
  208.3 75.5 %shard_map.326 = (bf16[4,256,512]{2,1,0:T(8,128)(2,1)}, f32[4,256,512]{2,1,0:T(8,128)}, bf16[512,1536]{1,0:T(8,128)(2,1)}, bf16[512,512]{1,0:T(8,128)(2,1)}, bf1...) custom-call(bf16[4,256,512]{2,1,0:T(8,128)(2,1)} %shard_map.325.refs, ...), custom_call_target="tpu_custom_call" | custom-call | flops 19327352832 | bytes 6291456 | tf_op jit(solution)/shard_map/pallas_call | solution.py:261
  283.8 2.7 convert_element_type.53.refs_1_
  286.5 86.2 %shard_map.327 = (bf16[4,256,512]{2,1,0:T(8,128)(2,1)}, f32[4,256,512]{2,1,0:T(8,128)}, bf16[512,1536]{1,0:T(8,128)(2,1)}, bf16[512,512]{1,0:T(8,128)(2,1)}, bf1...) custom-call(bf16[4,256,512]{2,1,0:T(8,128)(2,1)} %pad.42.refs_0_, ...), custom_call_target="tpu_custom_call" | custom-call | flops 19327352832 | bytes 6291456 | tf_op jit(solution)/shard_map/pallas_call | solution.py:261
  382.6 5.4 collective-permute-start.13
  389.2 3.1 collective-permute-start.15
  395.0 4.0 add_convert_fusion.2
  400.4 3.5 collective-permute-start.17
  407.3 4.7 add_convert_fusion.1
  413.6 3.2 collective-permute-start.19
  420.5 4.2 add_convert_fusion
  433.9 4.8 collective-permute-start.9
  438.8 2.4 copy.98
  445.3 2.4 copy.100
  447.7 5.5 collective-permute-start.11
  453.2 115.5 %all-reduce.18.cloned.1.call-done = f32[2,8848]{1,0:T(2,128)} async-done(((f32[2,8848]{1,0:T(2,128)}), f32[2,8848]{1,0:T(2,128)}) %all-reduce.18.cloned.1.call-update) | async-done | bytes 70800 | tf_op jit(solution)/shard_map/psum | solution.py:450
  572.4 5.8 broadcast_select_fusion
  578.2 5.5 maximum_select_fusion
  583.7 52.3 %all-reduce.22.cloned.1.call-done = (bf16[1,128,1536]{2,1,0:T(8,128)(2,1)}, bf16[1,128,512]{2,1,0:T(8,128)(2,1)}, bf16[1,128,2048]{2,1,0:T(8,128)(2,1)}, bf16[1,512,512]{2,1,0:T(8,128)(2,1)}) async-done(((bf16[1,128,1536]{2,1,0:T(8,128)(2,1)}, bf16[1,128,512]{2,1,0:T(8,128)(2,1)}, bf16[1,128,2048]{2,1,0:T(8,128)(2,1)}, bf16[1,512,512]{2,1,0:T(8,128)(2,1)}), (bf16[1,128,1536]{2,1,0:T(8,128)(2,1)}, ...) | async-done | bytes 1572880 | tf_op jit(solution)/shard_map/psum | solution.py:438
  (206 shorter events, 87.4 us)
Async XLA Ops:
  8.0 38.9 %all-reduce.20.cloned.1.call-start = ((), (), s32[]{:S(2)}) async-start(), calls=%async_computation.12 | async-start | bytes 147456
  17.8 43.6 %all-gather.9.cloned.1.call-start = ((), (), s32[]{:S(2)}) async-start(), calls=%async_computation.9 | async-start | bytes 1966080 | tf_op jit(solution)/shard_map/all_gather | solution.py:348
  18.4 90.0 %all-gather.11.cloned.1.call-start = ((), (), s32[]{:S(2)}) async-start(), calls=%async_computation.10 | async-start | bytes 2621440 | tf_op jit(solution)/shard_map/all_gather | solution.py:348
  19.0 135.2 %all-gather.13.cloned.1.call-start = ((), (), s32[]{:S(2)}) async-start(), calls=%async_computation.11 | async-start | bytes 2621440 | tf_op jit(solution)/shard_map/all_gather | solution.py:348
  19.5 549.1 %all-reduce.18.cloned.1.call-start = ((), (), s32[]{:S(2)}) async-start(), calls=%async_computation.4 | async-start | bytes 143360 | tf_op jit(solution)/shard_map/psum | solution.py:450
  40.7 74.7 %collective-permute-start.6 = (bf16[512,512]{1,0:T(8,128)(2,1)S(1)}, bf16[512,512]{1,0:T(8,128)(2,1)S(1)}, u32[]{:S(2)}, u32[]{:S(2)}) collective-permute-start(bf16[512,512]{1,0:T(8,128)(2,1)S(1)} %bitcast.116), channel_id=1, source_target_pairs={{16,0},{17,1},{18,2},{19,3},{20,4},{21,5},{22,6},{23,7},{24,8},{25... | collective-permute-start | bytes 1572872 | tf_op jit(solution)/shard_map/ppermute | solution.py:355
  61.4 94.1 %collective-permute-start.5 = (bf16[512,1536]{1,0:T(8,128)(2,1)}, bf16[512,1536]{1,0:T(8,128)(2,1)}, u32[]{:S(2)}, u32[]{:S(2)}) collective-permute-start(bf16[512,1536]{1,0:T(8,128)(2,1)} %bitcast.1), channel_id=1, source_target_pairs={{16,0},{17,1},{18,2},{19,3},{20,4},{21,5},{22,6},{23,7},{24,8},{25... | collective-permute-start | bytes 4718600 | tf_op jit(solution)/shard_map/ppermute | solution.py:355
  64.9 95.6 %collective-permute-start = (bf16[512,1536]{1,0:T(8,128)(2,1)}, bf16[512,1536]{1,0:T(8,128)(2,1)}, u32[]{:S(2)}, u32[]{:S(2)}) collective-permute-start(bf16[512,1536]{1,0:T(8,128)(2,1)} %bitcast.1), channel_id=1, source_target_pairs={{0,16},{1,17},{2,18},{3,19},{4,20},{5,21},{6,22},{7,23},{8,24},{9,... | collective-permute-start | bytes 4718600 | tf_op jit(solution)/shard_map/ppermute | solution.py:355
  108.3 56.1 %collective-permute-start.7 = (bf16[512,2048]{1,0:T(8,128)(2,1)}, bf16[512,2048]{1,0:T(8,128)(2,1)}, u32[]{:S(2)}, u32[]{:S(2)}) collective-permute-start(bf16[512,2048]{1,0:T(8,128)(2,1)} %bitcast.120), channel_id=1, source_target_pairs={{16,0},{17,1},{18,2},{19,3},{20,4},{21,5},{22,6},{23,7},{24,8},{25... | collective-permute-start | bytes 6291464 | tf_op jit(solution)/shard_map/ppermute | solution.py:355
  109.6 54.8 %collective-permute-start.2 = (bf16[512,2048]{1,0:T(8,128)(2,1)}, bf16[512,2048]{1,0:T(8,128)(2,1)}, u32[]{:S(2)}, u32[]{:S(2)}) collective-permute-start(bf16[512,2048]{1,0:T(8,128)(2,1)} %bitcast.121), channel_id=1, source_target_pairs={{0,16},{1,17},{2,18},{3,19},{4,20},{5,21},{6,22},{7,23},{8,24},{9,... | collective-permute-start | bytes 6291464 | tf_op jit(solution)/shard_map/ppermute | solution.py:355
  115.4 16.0 %collective-permute-start.1 = (bf16[512,512]{1,0:T(8,128)(2,1)S(1)}, bf16[512,512]{1,0:T(8,128)(2,1)}, u32[]{:S(2)}, u32[]{:S(2)}) collective-permute-start(bf16[512,512]{1,0:T(8,128)(2,1)S(1)} %bitcast.117), channel_id=1, source_target_pairs={{0,16},{1,17},{2,18},{3,19},{4,20},{5,21},{6,22},{7,23},{8,24},{9,... | collective-permute-start | bytes 1572872 | tf_op jit(solution)/shard_map/ppermute | solution.py:355
  154.2 14.5 %collective-permute-start.8 = (bf16[2048,512]{1,0:T(8,128)(2,1)}, bf16[2048,512]{1,0:T(8,128)(2,1)S(1)}, u32[]{:S(2)}, u32[]{:S(2)}) collective-permute-start(bf16[2048,512]{1,0:T(8,128)(2,1)} %bitcast.118), channel_id=1, source_target_pairs={{16,0},{17,1},{18,2},{19,3},{20,4},{21,5},{22,6},{23,7},{24,8},{25... | collective-permute-start | bytes 6291464 | tf_op jit(solution)/shard_map/ppermute | solution.py:355
  155.5 13.2 %collective-permute-start.3 = (bf16[2048,512]{1,0:T(8,128)(2,1)}, bf16[2048,512]{1,0:T(8,128)(2,1)S(1)}, u32[]{:S(2)}, u32[]{:S(2)}) collective-permute-start(bf16[2048,512]{1,0:T(8,128)(2,1)} %bitcast.119), channel_id=1, source_target_pairs={{0,16},{1,17},{2,18},{3,19},{4,20},{5,21},{6,22},{7,23},{8,24},{9,... | collective-permute-start | bytes 6291464 | tf_op jit(solution)/shard_map/ppermute | solution.py:355
  286.5 86.2 %copy-start.21 = (f32[1,1536]{1,0:T(1,128)S(1)}, f32[1,1536]{1,0:T(1,128)}, u32[]{:S(2)}) copy-start(f32[1,1536]{1,0:T(1,128)} %get-tuple-element.42) | copy-start | bytes 18436
  286.5 86.3 %copy-start.8 = (f32[4,128,512]{2,1,0:T(8,128)S(1)}, f32[4,128,512]{2,1,0:T(8,128)}, u32[]{:S(2)}) copy-start(f32[4,128,512]{2,1,0:T(8,128)} %get-tuple-element.44) | copy-start | bytes 3145732
  381.3 13.7 %collective-permute-start.12 = (bf16[512,1536]{1,0:T(8,128)(2,1)}, bf16[512,1536]{1,0:T(8,128)(2,1)}, u32[]{:S(2)}, u32[]{:S(2)}) collective-permute-start(bf16[512,1536]{1,0:T(8,128)(2,1)} %get-tuple-element.45), channel_id=1, source_target_pairs={{16,0},{17,1},{18,2},{19,3},{20,4},{21,5},{22,6},{23,7},{24,8},{25... | collective-permute-start | bytes 4718600 | tf_op jit(solution)/shard_map/ppermute | solution.py:355
  382.6 12.4 %collective-permute-start.13 = (bf16[512,1536]{1,0:T(8,128)(2,1)}, bf16[512,1536]{1,0:T(8,128)(2,1)}, u32[]{:S(2)}, u32[]{:S(2)}) collective-permute-start(bf16[512,1536]{1,0:T(8,128)(2,1)} %get-tuple-element.46), channel_id=1, source_target_pairs={{0,16},{1,17},{2,18},{3,19},{4,20},{5,21},{6,22},{7,23},{8,24},{9,... | collective-permute-start | bytes 4718600 | tf_op jit(solution)/shard_map/ppermute | solution.py:355
  387.9 5.2 collective-permute-start.14
  389.2 4.6 collective-permute-start.15
  393.1 179.2 %reduce-scatter.7.cloned.1.call-start = ((), (), s32[]{:S(2)}) async-start(), calls=%async_computation.6 | async-start | bytes 655360 | tf_op jit(solution)/shard_map/reduce_scatter | solution.py:436
  394.9 177.4 %reduce-scatter.5.cloned.1.call-start = ((), (), s32[]{:S(2)}) async-start(), calls=%async_computation.5 | async-start | bytes 1966080 | tf_op jit(solution)/shard_map/reduce_scatter | solution.py:436
  399.0 173.3 %reduce-scatter.9.cloned.1.call-start = ((), (), s32[]{:S(2)}) async-start(), calls=%async_computation.7 | async-start | bytes 2621440 | tf_op jit(solution)/shard_map/reduce_scatter | solution.py:436
  399.0 6.3 collective-permute-start.16
  400.4 6.9 %collective-permute-start.17 = (bf16[512,2048]{1,0:T(8,128)(2,1)S(1)}, bf16[512,2048]{1,0:T(8,128)(2,1)S(1)}, u32[]{:S(2)}, u32[]{:S(2)}) collective-permute-start(bf16[512,2048]{1,0:T(8,128)(2,1)S(1)} %copy-done.5), channel_id=1, source_target_pairs={{0,16},{1,17},{2,18},{3,19},{4,20},{5,21},{6,22},{7,23},{8,24},{9,... | collective-permute-start | bytes 6291464 | tf_op jit(solution)/shard_map/ppermute | solution.py:355
  412.1 160.3 %reduce-scatter.11.cloned.1.call-start = ((), (), s32[]{:S(2)}) async-start(), calls=%async_computation.8 | async-start | bytes 2621440 | tf_op jit(solution)/shard_map/reduce_scatter | solution.py:436
  412.1 6.4 collective-permute-start.18
  413.6 6.9 %collective-permute-start.19 = (bf16[2048,512]{1,0:T(8,128)(2,1)S(1)}, bf16[2048,512]{1,0:T(8,128)(2,1)S(1)}, u32[]{:S(2)}, u32[]{:S(2)}) collective-permute-start(bf16[2048,512]{1,0:T(8,128)(2,1)S(1)} %copy-done.2), channel_id=1, source_target_pairs={{0,16},{1,17},{2,18},{3,19},{4,20},{5,21},{6,22},{7,23},{8,24},{9,... | collective-permute-start | bytes 6291464 | tf_op jit(solution)/shard_map/ppermute | solution.py:355
  424.7 211.3 %all-reduce.22.cloned.1.call-start = ((), (), s32[]{:S(2)}) async-start(), calls=%async_computation.13 | async-start | bytes 3145728 | tf_op jit(solution)/shard_map/psum | solution.py:438
  427.9 144.4 %collective-permute-start.4 = (bf16[2,2,196,512]{3,1,2,0:T(2,128)(2,1)}, bf16[2,2,196,512]{3,1,2,0:T(2,128)(2,1)}, u32[]{:S(2)}, u32[]{:S(2)}) collective-permute-start(bf16[2,2,196,512]{3,1,2,0:T(2,128)(2,1)} %copy.88), channel_id=1, source_target_pairs={{16,0},{17,1},{18,2},{19,3},{20,4},{21,5},{22,6},{23,7},{24,8},{25... | collective-permute-start | bytes 2408456 | tf_op jit(solution)/shard_map/ppermute | solution.py:355
  433.9 138.5 %collective-permute-start.9 = (bf16[2,2,196,512]{3,1,2,0:T(2,128)(2,1)}, bf16[2,2,196,512]{3,1,2,0:T(2,128)(2,1)}, u32[]{:S(2)}, u32[]{:S(2)}) collective-permute-start(bf16[2,2,196,512]{3,1,2,0:T(2,128)(2,1)} %copy.96), channel_id=1, source_target_pairs={{0,16},{1,17},{2,18},{3,19},{4,20},{5,21},{6,22},{7,23},{8,24},{9,... | collective-permute-start | bytes 2408456 | tf_op jit(solution)/shard_map/ppermute | solution.py:355
  441.2 137.0 %collective-permute-start.10 = (f32[2,2,196,512]{3,1,2,0:T(2,128)}, f32[2,2,196,512]{3,1,2,0:T(2,128)}, u32[]{:S(2)}, u32[]{:S(2)}) collective-permute-start(f32[2,2,196,512]{3,1,2,0:T(2,128)} %copy.98), channel_id=1, source_target_pairs={{16,0},{17,1},{18,2},{19,3},{20,4},{21,5},{22,6},{23,7},{24,8},{25... | collective-permute-start | bytes 4816904 | tf_op jit(solution)/shard_map/ppermute | solution.py:355
  447.7 130.5 %collective-permute-start.11 = (f32[2,2,196,512]{3,1,2,0:T(2,128)}, f32[2,2,196,512]{3,1,2,0:T(2,128)}, u32[]{:S(2)}, u32[]{:S(2)}) collective-permute-start(f32[2,2,196,512]{3,1,2,0:T(2,128)} %copy.100), channel_id=1, source_target_pairs={{0,16},{1,17},{2,18},{3,19},{4,20},{5,21},{6,22},{7,23},{8,24},{9,... | collective-permute-start | bytes 4816904 | tf_op jit(solution)/shard_map/ppermute | solution.py:355
  (22 other events, 195.6 us)
Sparse Core Ops, SparseCore 0:
  17.9 20.3 all-reduce.19
  393.2 175.4 all-reduce.17
  572.5 63.4 all-reduce.21
Sparse Core Ops, SparseCore 1:
  19.8 41.5 all-gather.8
  62.8 45.5 all-gather.10
  109.8 44.3 all-gather.12
  396.7 20.4 reduce-scatter.6
  420.1 33.8 reduce-scatter.4
  456.2 42.9 reduce-scatter.8
  501.4 43.0 reduce-scatter.10

commit v2 on v1

--- a/solution.py
+++ b/solution.py
@@ -344,8 +344,13 @@
     table_rows = rel_table.shape[1]
     heads = rel_table.shape[2]
     hidden = fc1_bias.shape[1]
+
+    def quarter(part):
+        rows = part.shape[0] // lax.axis_size("rep")
+        return lax.dynamic_slice_in_dim(part, lax.axis_index("rep") * rows, rows, 0)
+
     own_mats = tuple(
-        lax.all_gather(part[0], "shard", axis=0, tiled=True)
+        lax.all_gather(quarter(part[0]), ("shard", "rep"), axis=0, tiled=True)
         for part in (w_qkv, w_proj, w_fc1, w_fc2)
     )
     from_zero = [(0, 1)]
@@ -433,9 +438,17 @@
         return (own + there).astype(jnp.bfloat16)
 
     big_total = jax.tree.map(summed, big_zero, big_there, big_one, sent_one[2])
-    owned = lax.psum_scatter(big_total, "shard", scatter_dimension=0, tiled=True)
+    n_shard, n_rep = lax.axis_size("shard"), lax.axis_size("rep")
+
+    def rep_major(part):
+        split = part.reshape(n_shard, n_rep, -1, part.shape[1]).transpose(1, 0, 2, 3)
+        return split.reshape(part.shape)
+
+    big_total = jax.tree.map(rep_major, big_total)
+    over_rep = lax.psum_scatter(big_total, "rep", scatter_dimension=0, tiled=True)
+    owned = lax.psum_scatter(over_rep, "shard", scatter_dimension=0, tiled=True)
     rows_qkv, rows_proj, rows_fc1, rows_fc2 = jax.tree.map(
-        lambda part: part.astype(jnp.float32), lax.psum(owned, "rep")
+        lambda part: part.astype(jnp.float32), lax.all_gather(owned, "rep", axis=0, tiled=True)
     )
 
     def small_grads(res):

time: 658 us -> 810 us (1.23)
  waiting for transfers between devices: 243 us -> 325 us
  blocking collectives: 21.1 us -> 88.2 us
  local copies, waits for them, and re-layouts: 54.5 us -> 68.1 us
  Pallas kernels: 199 us -> 189 us
    reduce_scatter x4 -> x8, waiting for transfers between devices: 0.04 us -> 139 us  [the longest x4 78.2 us: shards(): lax.psum_scatter(big_total, 'rep', scatter_dimension=0, tiled=True)]
    all_gather x1 -> x5, blocking collectives: 21.1 us -> 88.2 us  [the longest x1 46.3 us: shards(): lax.all_gather(quarter(part[0]), ('shard', 'rep'), axis=0, tiled=True)]
    psum x1 -> x0, waiting for transfers between devices: 52.3 us -> none  [shards(): lax.psum(owned, 'rep')]
    all_gather x3, waiting for transfers between devices: 66 us -> 93.1 us  [shards(): lax.all_gather(quarter(part[0]), ('shard', 'rep'), axis=0, tiled=True)]
    psum x1, waiting for transfers between devices: 116 us -> 91.1 us  [shards(): lax.psum(jnp.stack([small_grads(res_zero), small_grads(res_one)]), ('sect...]
    pallas_call x3, Pallas kernels: 199 us -> 189 us  [call_layer(): pl.pallas_call(functools.partial(layer_kernel, backward), out_shape=outs,...]
  transfers between devices with their start and end apart: 30 -> 33, of which waited for: 10 -> 12; matrix products, arithmetic and copies ran while one was open for 13% -> 13% of each run, Pallas kernels for 0% -> 0%
where the time goes in v2:
time: 810 us; the launch traced here: 802 us
  waiting for transfers between devices  325 us (40%)
  Pallas kernels  189 us (23%)
  blocking collectives  88.2 us (11%)
  local copies, waits for them, and re-layouts  68.1 us (8%)
  starting transfers between devices  60.7 us (7%)
  other arithmetic  46.5 us (6%)
  between operations  17.6 us (2%)
    pallas_call x3, Pallas kernels, call_layer(): pl.pallas_call(functools.partial(layer_kernel, backward), out_shape=outs,...  189 us
    all_gather x3, waiting for transfers between devices, shards(): lax.all_gather(quarter(part[0]), ('shard', 'rep'), axis=0, tiled=True)  93.1 us
    psum x1, waiting for transfers between devices, shards(): lax.psum(jnp.stack([small_grads(res_zero), small_grads(res_one)]), ('sect...  91.1 us
    reduce_scatter x4, waiting for transfers between devices, shards(): lax.psum_scatter(big_total, 'rep', scatter_dimension=0, tiled=True)  78.2 us
    reduce_scatter x4, waiting for transfers between devices, shards(): owned = lax.psum_scatter(over_rep, 'shard', scatter_dimension=0, tiled=True)  60.4 us
    ppermute x20, starting transfers between devices, moved(): return jax.tree.map(lambda part: lax.ppermute(part, 'section', route), tree)  60.1 us
    all_gather x1, blocking collectives, shards(): lax.all_gather(quarter(part[0]), ('shard', 'rep'), axis=0, tiled=True)  46.3 us
    all_gather x4, blocking collectives, shards(): lax.all_gather(owned, 'rep', axis=0, tiled=True)  41.9 us
  transfers between devices with their start and end apart: 33, of which 12 were waited for; matrix products, arithmetic and copies ran while one was open for 13% of the time, Pallas kernels for 0%

profile of v2, /device:TPU:0, one launch (start us, length us, event | category | flops | bytes accessed | tf_op | source)
XLA Modules:
  0.0 801.5 jit_solution(13449803303040993317)
XLA Ops:
  22.7 46.3 %all-gather.2 = bf16[1,512,512]{2,1,0:T(8,128)(2,1)S(1)} all-gather(bf16[1,32,512]{2,1,0:T(8,128)(2,1)S(1)} %constant_dynamic-slice_fusion.3), channel_id=4, replica_groups=mesh['section'=2,'shard'=4,'rep'=4] {'shard','rep'}, dimensions={1}, use_global_device_ids=true | all-gather | bytes 557056 | tf_op jit(solution)/shard_map/all_gather | solution.py:353
  87.9 5.3 collective-permute-start
  95.0 51.7 %all-gather.11.cloned.1.call-done = bf16[1,512,2048]{2,1,0:T(8,128)(2,1)} async-done(((bf16[1,32,2048]{2,1,0:T(8,128)(2,1)}), bf16[1,512,2048]{2,1,0:T(8,128)(2,1)}) %all-gather.11.cloned.1.call-update) | async-done | bytes 2097168 | tf_op jit(solution)/shard_map/all_gather | solution.py:353
  148.0 5.7 collective-permute-start.2
  157.3 4.3 copy.95
  169.7 39.7 %all-gather.13.cloned.1.call-done = bf16[1,2048,512]{2,1,0:T(8,128)(2,1)} async-done(((bf16[1,128,512]{2,1,0:T(8,128)(2,1)}), bf16[1,2048,512]{2,1,0:T(8,128)(2,1)}) %all-gather.13.cloned.1.call-update) | async-done | bytes 2097168 | tf_op jit(solution)/shard_map/all_gather | solution.py:353
  215.7 4.0 broadcast_select_fusion.5
  219.7 4.3 broadcast_select_fusion.3
  226.3 37.3 %shard_map.325.refs_0_ = bf16[4,256,512]{2,1,0:T(8,128)(2,1)} custom-call(bf16[4,256,512]{2,1,0:T(8,128)(2,1)} %pad.42.refs_0_, bf16[256,256]{1,0:T(8,128)(2,1)} %constant.47.clone.refs_1_.refs_2_, bf16[256,256]{1,0:T(8,128)(2,1)} %constant.48.clone.refs_2_.refs_3_, bf16[512,1536]{1,0:T(8,128)(2,1)} %get-tuple-element.100.refs_3_.refs_4_, ...), custom_call_target="tpu_custom_call" | custom-call | flops 6442450944 | bytes 6291456 | tf_op jit(solution)/shard_map/pallas_call | solution.py:261
  263.7 75.5 %shard_map.326 = (bf16[4,256,512]{2,1,0:T(8,128)(2,1)}, f32[4,256,512]{2,1,0:T(8,128)}, bf16[512,1536]{1,0:T(8,128)(2,1)}, bf16[512,512]{1,0:T(8,128)(2,1)}, bf1...) custom-call(bf16[4,256,512]{2,1,0:T(8,128)(2,1)} %shard_map.325.refs, ...), custom_call_target="tpu_custom_call" | custom-call | flops 19327352832 | bytes 6291456 | tf_op jit(solution)/shard_map/pallas_call | solution.py:261
  341.9 75.9 %shard_map.327 = (bf16[4,256,512]{2,1,0:T(8,128)(2,1)}, f32[4,256,512]{2,1,0:T(8,128)}, bf16[512,1536]{1,0:T(8,128)(2,1)}, bf16[512,512]{1,0:T(8,128)(2,1)}, bf1...) custom-call(bf16[4,256,512]{2,1,0:T(8,128)(2,1)} %pad.42.refs_0_, ...), custom_call_target="tpu_custom_call" | custom-call | flops 19327352832 | bytes 6291456 | tf_op jit(solution)/shard_map/pallas_call | solution.py:261
  419.1 5.4 collective-permute-start.13
  446.7 5.8 collective-permute-start.17
  456.2 4.0 add_convert_fusion.1
  463.2 5.7 collective-permute-start.19
  469.0 22.1 %reduce-scatter.9.cloned.1.call-done = bf16[128,1536]{1,0:T(8,128)(2,1)} async-done(((bf16[512,1536]{1,0:T(8,128)(2,1)}), bf16[128,1536]{1,0:T(8,128)(2,1)}) %reduce-scatter.9.cloned.1.call-update) | async-done | bytes 393232 | tf_op jit(solution)/shard_map/reduce_scatter | solution.py:448
  491.2 3.4 add_convert_fusion
  504.7 5.1 collective-permute-start.9
  519.7 5.4 collective-permute-start.11
  525.1 91.1 %all-reduce.16.cloned.1.call-done = f32[2,8848]{1,0:T(2,128)} async-done(((f32[2,8848]{1,0:T(2,128)}), f32[2,8848]{1,0:T(2,128)}) %all-reduce.16.cloned.1.call-update) | async-done | bytes 70800 | tf_op jit(solution)/shard_map/psum | solution.py:463
  619.9 5.7 broadcast_select_fusion
  625.6 31.0 %reduce-scatter.17.cloned.1.call-done = bf16[128,2048]{1,0:T(8,128)(2,1)} async-done(((bf16[512,2048]{1,0:T(8,128)(2,1)}), bf16[128,2048]{1,0:T(8,128)(2,1)}) %reduce-scatter.17.cloned.1.call-update) | async-done | bytes 524304 | tf_op jit(solution)/shard_map/reduce_scatter | solution.py:448
  656.6 5.8 maximum_select_fusion
  662.4 15.4 %reduce-scatter.15.cloned.1.call-done = bf16[32,512]{1,0:T(8,128)(2,1)} async-done(((bf16[128,512]{1,0:T(8,128)(2,1)}), bf16[32,512]{1,0:T(8,128)(2,1)}) %reduce-scatter.15.cloned.1.call-update) | async-done | bytes 32784 | tf_op jit(solution)/shard_map/reduce_scatter | solution.py:449
  677.8 8.6 %all_gather.37 = bf16[128,512]{1,0:T(8,128)(2,1)S(1)} all-gather(bf16[32,512]{1,0:T(8,128)(2,1)} %reduce-scatter.15.cloned.1.call-done), channel_id=1, replica_groups=mesh['section'=2,'shard'=4,'rep'=4] {'rep'}, dimensions={0}, use_global_device_ids=true | all-gather | bytes 163840 | tf_op jit(solution)/shard_map/all_gather | solution.py:451
  687.1 11.9 %reduce-scatter.11.cloned.1.call-done = bf16[32,1536]{1,0:T(8,128)(2,1)} async-done(((bf16[128,1536]{1,0:T(8,128)(2,1)}), bf16[32,1536]{1,0:T(8,128)(2,1)}) %reduce-scatter.11.cloned.1.call-update) | async-done | bytes 98320 | tf_op jit(solution)/shard_map/reduce_scatter | solution.py:449
  699.0 11.3 %all_gather.36 = bf16[128,1536]{1,0:T(8,128)(2,1)S(1)} all-gather(bf16[32,1536]{1,0:T(8,128)(2,1)} %reduce-scatter.11.cloned.1.call-done), channel_id=1, replica_groups=mesh['section'=2,'shard'=4,'rep'=4] {'rep'}, dimensions={0}, use_global_device_ids=true | all-gather | bytes 491520 | tf_op jit(solution)/shard_map/all_gather | solution.py:451
  710.4 25.1 %reduce-scatter.21.cloned.1.call-done = bf16[512,512]{1,0:T(8,128)(2,1)} async-done(((bf16[2048,512]{1,0:T(8,128)(2,1)}), bf16[512,512]{1,0:T(8,128)(2,1)}) %reduce-scatter.21.cloned.1.call-update) | async-done | bytes 524304 | tf_op jit(solution)/shard_map/reduce_scatter | solution.py:448
  736.5 23.1 %reduce-scatter.19.cloned.1.call-done = bf16[32,2048]{1,0:T(8,128)(2,1)} async-done(((bf16[128,2048]{1,0:T(8,128)(2,1)}), bf16[32,2048]{1,0:T(8,128)(2,1)}) %reduce-scatter.19.cloned.1.call-update) | async-done | bytes 131088 | tf_op jit(solution)/shard_map/reduce_scatter | solution.py:449
  759.5 11.0 %all_gather.38 = bf16[128,2048]{1,0:T(8,128)(2,1)S(1)} all-gather(bf16[32,2048]{1,0:T(8,128)(2,1)} %reduce-scatter.19.cloned.1.call-done), channel_id=1, replica_groups=mesh['section'=2,'shard'=4,'rep'=4] {'rep'}, dimensions={0}, use_global_device_ids=true | all-gather | bytes 655360 | tf_op jit(solution)/shard_map/all_gather | solution.py:451
  771.6 10.1 %reduce-scatter.23.cloned.1.call-done = bf16[128,512]{1,0:T(8,128)(2,1)} async-done(((bf16[512,512]{1,0:T(8,128)(2,1)}), bf16[128,512]{1,0:T(8,128)(2,1)}) %reduce-scatter.23.cloned.1.call-update) | async-done | bytes 131088 | tf_op jit(solution)/shard_map/reduce_scatter | solution.py:449
  781.6 11.0 %all_gather.39 = bf16[512,512]{1,0:T(8,128)(2,1)S(1)} all-gather(bf16[128,512]{1,0:T(8,128)(2,1)} %reduce-scatter.23.cloned.1.call-done), channel_id=1, replica_groups=mesh['section'=2,'shard'=4,'rep'=4] {'rep'}, dimensions={0}, use_global_device_ids=true | all-gather | bytes 655360 | tf_op jit(solution)/shard_map/all_gather | solution.py:451
  (223 shorter events, 115.8 us)
Async XLA Ops:
  8.0 67.2 %all-reduce.18.cloned.1.call-start = ((), (), s32[]{:S(2)}) async-start(), calls=%async_computation.20 | async-start | bytes 147456
  17.8 66.6 %all-gather.9.cloned.1.call-start = ((), (), s32[]{:S(2)}) async-start(), calls=%async_computation.17 | async-start | bytes 1671168 | tf_op jit(solution)/shard_map/all_gather | solution.py:353
  19.5 127.3 %all-gather.11.cloned.1.call-start = ((), (), s32[]{:S(2)}) async-start(), calls=%async_computation.18 | async-start | bytes 2228224 | tf_op jit(solution)/shard_map/all_gather | solution.py:353
  20.2 189.2 %all-gather.13.cloned.1.call-start = ((), (), s32[]{:S(2)}) async-start(), calls=%async_computation.19 | async-start | bytes 2228224 | tf_op jit(solution)/shard_map/all_gather | solution.py:353
  21.9 447.0 %reduce-scatter.13.cloned.1.call-start = ((), (), s32[]{:S(2)}) async-start(), calls=%async_computation.11 | async-start | bytes 655360 | tf_op jit(solution)/shard_map/reduce_scatter | solution.py:448
  69.0 84.7 %collective-permute-start.6 = (bf16[512,512]{1,0:T(8,128)(2,1)S(1)}, bf16[512,512]{1,0:T(8,128)(2,1)S(1)}, u32[]{:S(2)}, u32[]{:S(2)}) collective-permute-start(bf16[512,512]{1,0:T(8,128)(2,1)S(1)} %bitcast.147), channel_id=1, source_target_pairs={{16,0},{17,1},{18,2},{19,3},{20,4},{21,5},{22,6},{23,7},{24,8},{25... | collective-permute-start | bytes 1572872 | tf_op jit(solution)/shard_map/ppermute | solution.py:360
  84.4 126.3 %collective-permute-start.5 = (bf16[512,1536]{1,0:T(8,128)(2,1)}, bf16[512,1536]{1,0:T(8,128)(2,1)}, u32[]{:S(2)}, u32[]{:S(2)}) collective-permute-start(bf16[512,1536]{1,0:T(8,128)(2,1)} %bitcast.1), channel_id=1, source_target_pairs={{16,0},{17,1},{18,2},{19,3},{20,4},{21,5},{22,6},{23,7},{24,8},{25... | collective-permute-start | bytes 4718600 | tf_op jit(solution)/shard_map/ppermute | solution.py:360
  87.9 127.8 %collective-permute-start = (bf16[512,1536]{1,0:T(8,128)(2,1)}, bf16[512,1536]{1,0:T(8,128)(2,1)}, u32[]{:S(2)}, u32[]{:S(2)}) collective-permute-start(bf16[512,1536]{1,0:T(8,128)(2,1)} %bitcast.1), channel_id=1, source_target_pairs={{0,16},{1,17},{2,18},{3,19},{4,20},{5,21},{6,22},{7,23},{8,24},{9,... | collective-permute-start | bytes 4718600 | tf_op jit(solution)/shard_map/ppermute | solution.py:360
  146.7 73.0 %collective-permute-start.7 = (bf16[512,2048]{1,0:T(8,128)(2,1)}, bf16[512,2048]{1,0:T(8,128)(2,1)}, u32[]{:S(2)}, u32[]{:S(2)}) collective-permute-start(bf16[512,2048]{1,0:T(8,128)(2,1)} %bitcast.150), channel_id=1, source_target_pairs={{16,0},{17,1},{18,2},{19,3},{20,4},{21,5},{22,6},{23,7},{24,8},{25... | collective-permute-start | bytes 6291464 | tf_op jit(solution)/shard_map/ppermute | solution.py:360
  148.0 71.7 %collective-permute-start.2 = (bf16[512,2048]{1,0:T(8,128)(2,1)}, bf16[512,2048]{1,0:T(8,128)(2,1)}, u32[]{:S(2)}, u32[]{:S(2)}) collective-permute-start(bf16[512,2048]{1,0:T(8,128)(2,1)} %bitcast.151), channel_id=1, source_target_pairs={{0,16},{1,17},{2,18},{3,19},{4,20},{5,21},{6,22},{7,23},{8,24},{9,... | collective-permute-start | bytes 6291464 | tf_op jit(solution)/shard_map/ppermute | solution.py:360
  153.8 15.9 %collective-permute-start.1 = (bf16[512,512]{1,0:T(8,128)(2,1)S(1)}, bf16[512,512]{1,0:T(8,128)(2,1)}, u32[]{:S(2)}, u32[]{:S(2)}) collective-permute-start(bf16[512,512]{1,0:T(8,128)(2,1)S(1)} %bitcast.148), channel_id=1, source_target_pairs={{0,16},{1,17},{2,18},{3,19},{4,20},{5,21},{6,22},{7,23},{8,24},{9,... | collective-permute-start | bytes 1572872 | tf_op jit(solution)/shard_map/ppermute | solution.py:360
  209.4 14.6 %collective-permute-start.8 = (bf16[2048,512]{1,0:T(8,128)(2,1)}, bf16[2048,512]{1,0:T(8,128)(2,1)S(1)}, u32[]{:S(2)}, u32[]{:S(2)}) collective-permute-start(bf16[2048,512]{1,0:T(8,128)(2,1)} %bitcast.152), channel_id=1, source_target_pairs={{16,0},{17,1},{18,2},{19,3},{20,4},{21,5},{22,6},{23,7},{24,8},{25... | collective-permute-start | bytes 6291464 | tf_op jit(solution)/shard_map/ppermute | solution.py:360
  210.7 13.3 %collective-permute-start.3 = (bf16[2048,512]{1,0:T(8,128)(2,1)}, bf16[2048,512]{1,0:T(8,128)(2,1)S(1)}, u32[]{:S(2)}, u32[]{:S(2)}) collective-permute-start(bf16[2048,512]{1,0:T(8,128)(2,1)} %bitcast.153), channel_id=1, source_target_pairs={{0,16},{1,17},{2,18},{3,19},{4,20},{5,21},{6,22},{7,23},{8,24},{9,... | collective-permute-start | bytes 6291464 | tf_op jit(solution)/shard_map/ppermute | solution.py:360
  417.8 18.4 %collective-permute-start.12 = (bf16[512,1536]{1,0:T(8,128)(2,1)}, bf16[512,1536]{1,0:T(8,128)(2,1)}, u32[]{:S(2)}, u32[]{:S(2)}) collective-permute-start(bf16[512,1536]{1,0:T(8,128)(2,1)} %get-tuple-element.45), channel_id=1, source_target_pairs={{16,0},{17,1},{18,2},{19,3},{20,4},{21,5},{22,6},{23,7},{24,8},{25... | collective-permute-start | bytes 4718600 | tf_op jit(solution)/shard_map/ppermute | solution.py:360
  419.1 17.1 %collective-permute-start.13 = (bf16[512,1536]{1,0:T(8,128)(2,1)}, bf16[512,1536]{1,0:T(8,128)(2,1)}, u32[]{:S(2)}, u32[]{:S(2)}) collective-permute-start(bf16[512,1536]{1,0:T(8,128)(2,1)} %get-tuple-element.46), channel_id=1, source_target_pairs={{0,16},{1,17},{2,18},{3,19},{4,20},{5,21},{6,22},{7,23},{8,24},{9,... | collective-permute-start | bytes 4718600 | tf_op jit(solution)/shard_map/ppermute | solution.py:360
  425.8 4.6 collective-permute-start.15
  432.6 58.5 %reduce-scatter.9.cloned.1.call-start = ((), (), s32[]{:S(2)}) async-start(), calls=%async_computation.9 | async-start | bytes 1966080 | tf_op jit(solution)/shard_map/reduce_scatter | solution.py:448
  440.5 175.8 %all-reduce.16.cloned.1.call-start = ((), (), s32[]{:S(2)}) async-start(), calls=%async_computation.8 | async-start | bytes 143360 | tf_op jit(solution)/shard_map/psum | solution.py:463
  445.4 10.8 %collective-permute-start.16 = (bf16[512,2048]{1,0:T(8,128)(2,1)}, bf16[512,2048]{1,0:T(8,128)(2,1)}, u32[]{:S(2)}, u32[]{:S(2)}) collective-permute-start(bf16[512,2048]{1,0:T(8,128)(2,1)} %get-tuple-element.49), channel_id=1, source_target_pairs={{16,0},{17,1},{18,2},{19,3},{20,4},{21,5},{22,6},{23,7},{24,8},{25... | collective-permute-start | bytes 6291464 | tf_op jit(solution)/shard_map/ppermute | solution.py:360
  446.7 9.5 %collective-permute-start.17 = (bf16[512,2048]{1,0:T(8,128)(2,1)}, bf16[512,2048]{1,0:T(8,128)(2,1)}, u32[]{:S(2)}, u32[]{:S(2)}) collective-permute-start(bf16[512,2048]{1,0:T(8,128)(2,1)} %get-tuple-element.50), channel_id=1, source_target_pairs={{0,16},{1,17},{2,18},{3,19},{4,20},{5,21},{6,22},{7,23},{8,24},{9,... | collective-permute-start | bytes 6291464 | tf_op jit(solution)/shard_map/ppermute | solution.py:360
  456.1 200.4 %reduce-scatter.17.cloned.1.call-start = ((), (), s32[]{:S(2)}) async-start(), calls=%async_computation.13 | async-start | bytes 2621440 | tf_op jit(solution)/shard_map/reduce_scatter | solution.py:448
  461.7 216.1 %reduce-scatter.15.cloned.1.call-start = ((), (), s32[]{:S(2)}) async-start(), calls=%async_computation.12 | async-start | bytes 163840 | tf_op jit(solution)/shard_map/reduce_scatter | solution.py:449
  461.7 29.5 %collective-permute-start.18 = (bf16[2048,512]{1,0:T(8,128)(2,1)}, bf16[2048,512]{1,0:T(8,128)(2,1)}, u32[]{:S(2)}, u32[]{:S(2)}) collective-permute-start(bf16[2048,512]{1,0:T(8,128)(2,1)} %get-tuple-element.51), channel_id=1, source_target_pairs={{16,0},{17,1},{18,2},{19,3},{20,4},{21,5},{22,6},{23,7},{24,8},{25... | collective-permute-start | bytes 6291464 | tf_op jit(solution)/shard_map/ppermute | solution.py:360
  463.2 28.0 %collective-permute-start.19 = (bf16[2048,512]{1,0:T(8,128)(2,1)S(1)}, bf16[2048,512]{1,0:T(8,128)(2,1)}, u32[]{:S(2)}, u32[]{:S(2)}) collective-permute-start(bf16[2048,512]{1,0:T(8,128)(2,1)S(1)} %copy-done.4), channel_id=1, source_target_pairs={{0,16},{1,17},{2,18},{3,19},{4,20},{5,21},{6,22},{7,23},{8,24},{9,... | collective-permute-start | bytes 6291464 | tf_op jit(solution)/shard_map/ppermute | solution.py:360
  468.9 230.1 %reduce-scatter.11.cloned.1.call-start = ((), (), s32[]{:S(2)}) async-start(), calls=%async_computation.10 | async-start | bytes 491520 | tf_op jit(solution)/shard_map/reduce_scatter | solution.py:449
  491.2 244.3 %reduce-scatter.21.cloned.1.call-start = ((), (), s32[]{:S(2)}) async-start(), calls=%async_computation.15 | async-start | bytes 2621440 | tf_op jit(solution)/shard_map/reduce_scatter | solution.py:448
  496.2 263.3 %reduce-scatter.19.cloned.1.call-start = ((), (), s32[]{:S(2)}) async-start(), calls=%async_computation.14 | async-start | bytes 655360 | tf_op jit(solution)/shard_map/reduce_scatter | solution.py:449
  499.7 120.2 %collective-permute-start.4 = (bf16[2,2,196,512]{3,1,2,0:T(2,128)(2,1)}, bf16[2,2,196,512]{3,1,2,0:T(2,128)(2,1)}, u32[]{:S(2)}, u32[]{:S(2)}) collective-permute-start(bf16[2,2,196,512]{3,1,2,0:T(2,128)(2,1)} %copy.96), channel_id=1, source_target_pairs={{16,0},{17,1},{18,2},{19,3},{20,4},{21,5},{22,6},{23,7},{24,8},{25... | collective-permute-start | bytes 2408456 | tf_op jit(solution)/shard_map/ppermute | solution.py:360
  504.7 115.2 %collective-permute-start.9 = (bf16[2,2,196,512]{3,1,2,0:T(2,128)(2,1)}, bf16[2,2,196,512]{3,1,2,0:T(2,128)(2,1)}, u32[]{:S(2)}, u32[]{:S(2)}) collective-permute-start(bf16[2,2,196,512]{3,1,2,0:T(2,128)(2,1)} %copy.104), channel_id=1, source_target_pairs={{0,16},{1,17},{2,18},{3,19},{4,20},{5,21},{6,22},{7,23},{8,24},{9,... | collective-permute-start | bytes 2408456 | tf_op jit(solution)/shard_map/ppermute | solution.py:360
  512.3 144.3 %collective-permute-start.10 = (f32[2,2,196,512]{3,1,2,0:T(2,128)}, f32[2,2,196,512]{3,1,2,0:T(2,128)}, u32[]{:S(2)}, u32[]{:S(2)}) collective-permute-start(f32[2,2,196,512]{3,1,2,0:T(2,128)} %copy.106), channel_id=1, source_target_pairs={{16,0},{17,1},{18,2},{19,3},{20,4},{21,5},{22,6},{23,7},{24,8},{25... | collective-permute-start | bytes 4816904 | tf_op jit(solution)/shard_map/ppermute | solution.py:360
  519.7 136.9 %collective-permute-start.11 = (f32[2,2,196,512]{3,1,2,0:T(2,128)}, f32[2,2,196,512]{3,1,2,0:T(2,128)}, u32[]{:S(2)}, u32[]{:S(2)}) collective-permute-start(f32[2,2,196,512]{3,1,2,0:T(2,128)} %copy.108), channel_id=1, source_target_pairs={{0,16},{1,17},{2,18},{3,19},{4,20},{5,21},{6,22},{7,23},{8,24},{9,... | collective-permute-start | bytes 4816904 | tf_op jit(solution)/shard_map/ppermute | solution.py:360
  656.5 125.1 %reduce-scatter.23.cloned.1.call-start = ((), (), s32[]{:S(2)}) async-start(), calls=%async_computation.16 | async-start | bytes 655360 | tf_op jit(solution)/shard_map/reduce_scatter | solution.py:449
  (23 other events, 293.7 us)
Sparse Core Ops, SparseCore 0:
  18.0 20.3 all-reduce.17
  432.7 23.5 reduce-scatter.12
  460.2 30.9 reduce-scatter.8
  498.1 118.1 all-reduce.15
  619.4 37.1 reduce-scatter.16
  658.6 19.1 reduce-scatter.14
  680.2 18.7 reduce-scatter.10
  702.0 33.4 reduce-scatter.20
  737.9 21.6 reduce-scatter.18
  761.8 19.8 reduce-scatter.22
Sparse Core Ops, SparseCore 1:
  21.7 62.7 all-gather.8
  87.6 59.0 all-gather.10
  149.9 59.4 all-gather.12
